TPU v7x, 32 devices: a whole 2x2x4 slice. The times are simulated.
32 devices in a mesh: shard: 4 (over z), rep: 8 (over y, x, core).
Axes of the slice: x: 2, y: 2, z: 4, core: 2. Of those that a mesh axis runs over, the one named last changes fastest.
Arguments:
- tokens: bfloat16 [128, 256, 384], P(('shard', 'rep')), may hold values from -6 to 6
- condition: bfloat16 [128, 384], P(('shard', 'rep')), may hold values from -6 to 6
- cotangent: bfloat16 [128, 256, 384], P(('shard', 'rep')), may hold values from -6 to 6
- attend_weight: float32 [384, 1152], P(None, 'shard'), may hold values from -0.3125 to 0.3125
- project_weight: float32 [384, 384], P(None, 'shard'), may hold values from -1.75 to 1.75
- expand_weight: float32 [384, 1536], P(None, 'shard'), may hold values from -0.3125 to 0.3125
- contract_weight: float32 [384, 1536], P(None, 'shard'), may hold values from -0.15625 to 0.15625
- modulate_weight: float32 [384, 2304], P(None, 'shard'), may hold values from -0.3125 to 0.3125
- biases: float32 [4224], P('shard'), may hold values from -1.2 to 1.2
- attend_moment: float32 [384, 1152], P(None, 'shard'), may hold values from -2606.6784 to 2606.6784
- project_moment: float32 [384, 384], P(None, 'shard'), may hold values from -488.7522 to 488.7522
- expand_moment: float32 [384, 1536], P(None, 'shard'), may hold values from -814.58701 to 814.58701
- contract_moment: float32 [384, 1536], P(None, 'shard'), may hold values from -1629.17402 to 1629.17402
- modulate_moment: float32 [384, 2304], P(None, 'shard'), may hold values from -1955.0088 to 1955.0088
- bias_first: float32 [4224], P('shard'), may hold values from -121.282955 to 121.282955
- bias_second: float32 [4224], P('shard'), may hold values from 0.65536 to 262.144, as said below
Outputs:
- block_output: bfloat16 [128, 256, 384], P(('shard', 'rep'))
- tokens_grad: float32 [128, 256, 384], P(('shard', 'rep'))
- condition_grad: float32 [128, 384], P(('shard', 'rep'))
- attend_grad: float32 [384, 1152], P(None, 'shard')
- project_grad: float32 [384, 384], P(None, 'shard')
- expand_grad: float32 [384, 1536], P(None, 'shard')
- contract_grad: float32 [384, 1536], P(None, 'shard')
- modulate_grad: float32 [384, 2304], P(None, 'shard')
- attend_momentum: float32 [384, 1152], P(None, 'shard')
- project_momentum: float32 [384, 384], P(None, 'shard')
- expand_momentum: float32 [384, 1536], P(None, 'shard')
- contract_momentum: float32 [384, 1536], P(None, 'shard')
- modulate_momentum: float32 [384, 2304], P(None, 'shard')
- attend_updated: float32 [384, 1152], P(None, 'shard')
- project_updated: float32 [384, 384], P(None, 'shard')
- expand_updated: float32 [384, 1536], P(None, 'shard')
- contract_updated: float32 [384, 1536], P(None, 'shard')
- modulate_updated: float32 [384, 2304], P(None, 'shard')
- bias_gradient: float32 [4224], P('shard')
- bias_momentum: float32 [4224], P('shard')
- bias_variance: float32 [4224], P('shard')
- bias_updated: float32 [4224], P('shard')
Inputs may be any that keep to these rules, and one draw needn't show every extreme that they name: `bias_second`: second moment of the biases, positive.
All inputs are finite; a program needn't handle non-finite values.
Results may differ from a plain program's by a relative error of at most 0.013.
The roundings to bfloat16 on the way count: a program that leaves them out, or rounds other values in their place, can miss the bound.
Values may be sent and summed in bfloat16 or wider, within the bound.
No kernel may reach another device: no remote copies, remote signals or barrier semaphores. Data moves between devices by JAX's collectives and lax.ppermute only.
A program may use at most 128 MiB of HBM per device.

v0:
```python
from functools import partial
import math

import jax
import jax.numpy as jnp
from jax import lax
from jax.experimental import pallas as pl
from jax.experimental.pallas import tpu as pltpu
from jax.sharding import PartitionSpec as P

D = 384
HEADS = 6
HEAD = 64
FF = 1536
LEN = 256
NS_ITERS = 5
STEP = 10
PAIR = 2 * HEAD
CHUNK = 512
GROUP = 8
BLOCK = 2
BIAS_LEN = 6 * D + FF + D
NOTE = 16
GRANTS = {
    "attention_forward": 40,
    "perceptron": 40,
    "attention_backward": 32,
    "attend_backward": 36,
    "momenta": 32,
    "gram": 24,
    "polynomial": 20,
    "update": 24,
}

POLY_LINEAR = 3.4445
POLY_CUBIC = -4.775
POLY_QUINTIC = 2.0315
MOMENTUM = 0.95
MUON_RATE = 0.4
WEIGHT_DECAY = 0.01
ADAM_RATE = 0.1
BETA_ONE = 0.9
BETA_TWO = 0.999
ADAM_EPSILON = 1e-08
GELU_SLOPE = math.sqrt(2.0 / math.pi)
GELU_CUBIC = 0.044715

LOW = jnp.bfloat16
FULL = jnp.float32

SLOTS = ((4, 0), (4, 1), (0, 0), (2, 0), (2, 1), (3, 0), (3, 1), (1, 0))


def shift(value, distance):
    size = lax.axis_size("shard")
    return lax.ppermute(value, "shard", [(i, (i + distance) % size) for i in range(size)])


def flip(value, mask):
    size = lax.axis_size("rep")
    return lax.ppermute(value, "rep", [(i, i ^ mask) for i in range(size)])


def exchange(pieces):
    return [pieces[0]] + [shift(pieces[d], d) for d in range(1, len(pieces))]


def gather_chips(value):
    return [value] + [flip(value, 2 * t) for t in range(1, GROUP // 2)]


def gather_group(value):
    stacked = jnp.stack(gather_chips(value))
    return stacked, flip(stacked, 1)


def sum_cores(keep, send, ids, name, after):
    received = flip(send, 1)
    shape = keep.shape[1:]
    return local_call(
        split_sum,
        ids,
        [(keep, False), (received, False)],
        [(shape, FULL, False)] + [(shape, LOW, False)] * (keep.shape[0] - 1),
        [],
        1,
        keep.size,
        name,
        after=after,
    )


def exchange_chips(totals):
    return [totals[0]] + [flip(totals[t], 2 * t) for t in range(1, GROUP // 2)]


def sum_rest(value):
    for bit in range(3, lax.axis_size("rep").bit_length() - 1):
        value = (value.astype(FULL) + flip(value, 1 << bit).astype(FULL)).astype(LOW)
    return value


def dot(left, right):
    return lax.dot_general(left, right, (((1,), (0,)), ((), ())), preferred_element_type=FULL)


def dot_nt(left, right):
    return lax.dot_general(left, right, (((1,), (1,)), ((), ())), preferred_element_type=FULL)


def dot_tn(left, right):
    return lax.dot_general(left, right, (((0,), (0,)), ((), ())), preferred_element_type=FULL)


def split_low(value):
    high = value.astype(LOW)
    return high, (value - high.astype(FULL)).astype(LOW)


def dot_split(left, right, product=dot):
    return product(left[0], right[0]) + (product(left[0], right[1]) + product(left[1], right[0]))


def normalize(values):
    centered = values - jnp.mean(values, -1, keepdims=True)
    inverse_spread = lax.rsqrt(jnp.mean(centered * centered, -1, keepdims=True) + 1e-06)
    return centered * inverse_spread, inverse_spread


def normalize_back(upstream, normed, inverse_spread):
    return inverse_spread * (
        upstream
        - jnp.mean(upstream, -1, keepdims=True)
        - normed * jnp.mean(upstream * normed, -1, keepdims=True)
    )


def local_call(kernel, ids, inputs, outputs, scratch, steps, flops, name, after=()):
    def run(*refs):
        kernel(*refs[: 1 + len(inputs)], *refs[1 + len(inputs) + len(after) :])

    def spec(shape, blocked):
        zeros = (0,) * (len(shape) - 1)
        if isinstance(blocked, tuple):
            rows, place = blocked
            return pl.BlockSpec(
                (rows,) + tuple(shape[1:]), lambda i, ids: (place(ids[1]),) + zeros
            )
        if blocked:
            block = (shape[0] // steps,) + tuple(shape[1:])
            return pl.BlockSpec(block, lambda i, _: (i,) + zeros)
        return pl.BlockSpec(tuple(shape), lambda i, _: (0,) + zeros)

    moved = sum(v.size * v.dtype.itemsize for v, _ in inputs)
    moved += sum(math.prod(shape) * jnp.dtype(kind).itemsize for shape, kind, _ in outputs)
    return pl.pallas_call(
        run,
        grid_spec=pltpu.PrefetchScalarGridSpec(
            num_scalar_prefetch=1,
            grid=(steps,),
            in_specs=[spec(v.shape, blocked) for v, blocked in inputs]
            + [pl.BlockSpec(memory_space=pl.ANY) for _ in after],
            out_specs=[spec(shape, blocked) for shape, _, blocked in outputs],
            scratch_shapes=scratch,
        ),
        out_shape=[jax.ShapeDtypeStruct(shape, kind) for shape, kind, _ in outputs],
        compiler_params=pltpu.CompilerParams(
            dimension_semantics=("arbitrary",), vmem_limit_bytes=GRANTS.get(name, 16) * 1024 * 1024
        ),
        cost_estimate=pl.CostEstimate(flops=flops, bytes_accessed=moved, transcendentals=0),
        name=name,
    )(ids, *[v for v, _ in inputs], *after)


def pieces_of(ids, stacked, flipped):
    for t in range(GROUP // 2):
        for bit, blocks in enumerate((stacked, flipped)):
            yield ids[1] ^ (2 * t + bit), blocks.at[t]


def rows_at(place, rows):
    return pl.ds(pl.multiple_of(place * rows, rows), rows)


def turn(value):
    filled = value.shape[1]
    extra = -filled % 128
    if extra:
        value = jnp.concatenate([value, jnp.zeros((value.shape[0], extra), value.dtype)], axis=1)
    return value.T[:filled]


def head_masks(values):
    lane = lax.broadcasted_iota(jnp.int32, values.shape, 1) % PAIR
    zero = jnp.zeros_like(values)
    return (
        jnp.where(lane < HEAD, values, zero).astype(LOW),
        jnp.where(lane < HEAD, zero, values).astype(LOW),
    )


def split_sum(ids, keep, received, own, *others):
    own[...] = keep[0] + received[0].astype(FULL)
    for t, other in enumerate(others):
        other[...] = (keep[t + 1] + received[t + 1].astype(FULL)).astype(LOW)


def modulation_kernel(ids, *refs):
    shards = refs[-1].shape[0]
    notes, weight, answers, weight_low, stacked = (
        refs[:shards], refs[shards], refs[shards + 1 : -2], refs[-2], refs[-1],
    )
    low = weight[...].astype(LOW)
    weight_low[...] = low
    for d, (note, answer) in enumerate(zip(notes, answers)):
        answer[...] = dot_nt(note[:NOTE, :], low)[: answer.shape[0]]
        stacked[d] = note[NOTE:, :]


def total_kernel(ids, own, *refs):
    total = own[...]
    for piece in refs[:-1]:
        total = total + piece[...].astype(FULL)
    refs[-1][...] = total.astype(LOW)


def prepare(ids, condition, biases, attend, project, note, first):
    latents = condition.shape[0]
    value = condition[...].astype(FULL)
    first[...] = jnp.zeros_like(first)
    first[:latents, :] = value / (1.0 + jnp.exp(-value))
    share = biases.shape[1]
    for b in range(-(-share // D)):
        filled = min(D, share - b * D)
        first[latents + b : latents + b + 1, :filled] = biases[:, b * D : b * D + filled]
    note[:NOTE, :] = first[...].astype(LOW)

    @pl.when(ids[1] < 6)
    def _():
        note[NOTE:, :] = attend[...].astype(LOW)

    @pl.when(ids[1] >= 6)
    def _():
        note[NOTE:, :] = project[...].astype(LOW)


def pack(ids, *refs):
    start = 0
    for weight in refs[:-1]:
        width = weight.shape[1]
        refs[-1][:, start : start + width] = weight[...].astype(LOW)
        start = start + width


def stack(ids, *refs):
    for t, block in enumerate(refs[:-1]):
        refs[-1][t] = block[...]


def attention_forward(
    ids, tokens, stacked, flipped, *refs,
):
    shards = (len(refs) - 16) // 2
    answers, notes = refs[:shards], refs[shards : 2 * shards]
    (
        qkv, probs, attended, branch, wq, wo, mod_all, bias_up, bias_down,
        ordered, query_a, query_b, mod_parts, bias_parts, wq_plain, wo_plain,
    ) = refs[2 * shards :]
    rows = ordered.shape[1] // GROUP
    wide, narrow = 3 * D // shards, D // shards

    @pl.when(pl.program_id(0) == 0)
    def _():
        for place, block in pieces_of(ids, stacked, flipped):
            for d in range(shards):
                source = lax.rem(ids[0] - d + shards, shards)
                ordered[source, rows_at(place, rows), :] = block[d].astype(ordered.dtype)
        for s in range(shards):
            wq[s * wide : (s + 1) * wide, :] = ordered[s, :wide, :].astype(LOW)
            wo[s * narrow : (s + 1) * narrow, :] = ordered[s, wide:, :].astype(LOW)
        wq_plain[...] = wq[...].T
        wo_plain[...] = wo[...].T
        for d in range(shards):
            mod_parts[lax.rem(ids[0] + d, shards)] = answers[d][...]
            bias_parts[lax.rem(ids[0] - d + shards, shards)] = notes[d][:NOTE, :].astype(FULL)
        latents = mod_all.shape[0]
        share = BIAS_LEN // shards
        pieces = []
        for s in range(shards):
            for b in range(-(-share // D)):
                row = bias_parts[s, latents + b : latents + b + 1, :]
                pieces.append(row[:, : min(D, share - b * D)])
        bias = jnp.concatenate(pieces, axis=1)
        whole = jnp.concatenate([mod_parts[s] for s in range(shards)], axis=1) + bias[:, : 6 * D]
        for latent in range(latents):
            for b in range(6):
                mod_all[latent, b : b + 1, :] = whole[latent : latent + 1, b * D : (b + 1) * D]
        bias_up[...] = bias[:, 6 * D : 6 * D + FF]
        bias_down[...] = bias[:, 6 * D + FF :]

    count = tokens.shape[0]
    mod = mod_all[pl.ds(pl.program_id(0) * count, count)]
    normed, _ = normalize(tokens[...].astype(FULL))
    hidden = normed * (1.0 + mod[:, 1:2, :]) + mod[:, 0:1, :]
    hidden = hidden.reshape(count * LEN, D).astype(LOW)
    queries = dot(hidden, wq_plain[:, :D])
    masked_a, masked_b = head_masks(queries)
    query_a[...] = masked_a
    query_b[...] = masked_b
    qkv[:, :, :D] = queries.astype(LOW).reshape(count, LEN, D)
    qkv[:, :, D:] = dot(hidden, wq_plain[:, D:]).astype(LOW).reshape(count, LEN, 2 * D)

    @pl.loop(0, count)
    def _(latent):
        span = pl.ds(pl.multiple_of(latent * LEN, LEN), LEN)
        for pair in range(HEADS // 2):
            lanes = slice(pair * PAIR, (pair + 1) * PAIR)
            keys = qkv[latent, :, D + pair * PAIR : D + (pair + 1) * PAIR]
            values = qkv[latent, :, 2 * D + pair * PAIR : 2 * D + (pair + 1) * PAIR].T
            results = []
            for member, masked in enumerate((query_a, query_b)):
                scores = dot_nt(keys, masked[span, lanes]) * (HEAD ** (-0.5) / math.log(2.0))
                top = jnp.max(scores, 0, keepdims=True)
                raised = jnp.exp2(scores - top)
                share = (raised * (1.0 / jnp.sum(raised, 0, keepdims=True))).astype(LOW)
                probs[latent, 2 * pair + member] = share
                results.append(dot(values[member * HEAD : (member + 1) * HEAD], share))
            attended[latent, :, lanes] = jnp.concatenate(results, axis=0).T.astype(LOW)

    branch[...] = dot(attended[...].reshape(count * LEN, D), wo_plain[...]).reshape(count, LEN, D)


def perceptron(
    ids, tokens, branch, mod, cotangent, stacked, flipped, bias_up, bias_down,
    out, grad_mixed, grad_mod, keep, send, sum_up, sum_down,
    ordered, wu, wd, act, slope, total_up, total_down,
):
    shards = ordered.shape[0]
    rows = D // GROUP
    width = FF // shards
    step = pl.program_id(0)

    @pl.when(step == 0)
    def _():
        for place, block in pieces_of(ids, stacked, flipped):
            for d in range(shards):
                source = lax.rem(ids[0] - d + shards, shards)
                ordered[source, rows_at(place, rows), :] = block[d]
        for i in range(GROUP):
            span = slice(i * rows, (i + 1) * rows)
            pieces = [ordered[s, span, :] for s in range(shards)]
            wu[span, :] = jnp.concatenate([p[:, :width] for p in pieces], axis=1)
            wd[span, :] = jnp.concatenate([p[:, width:] for p in pieces], axis=1)
        total_up[...] = jnp.zeros_like(total_up)
        total_down[...] = jnp.zeros_like(total_down)
        sum_up[...] = jnp.zeros_like(sum_up)
        sum_down[...] = jnp.zeros_like(sum_down)

    count = tokens.shape[0]
    flat = count * LEN
    branch_out = branch[...]
    mixed = tokens[...].astype(FULL) + mod[:, 2:3, :] * branch_out
    normed, inverse_spread = normalize(mixed)
    hidden = (normed * (1.0 + mod[:, 4:5, :]) + mod[:, 3:4, :]).reshape(flat, D).astype(LOW)
    result = jnp.zeros((flat, D), FULL)
    for start in range(0, FF, CHUNK):
        span = slice(start, start + CHUNK)
        u = dot(hidden, wu[:, span]) + bias_up[:, span]
        square = u * u
        half = 0.5 + 0.5 * jnp.tanh(u * (GELU_SLOPE + (GELU_SLOPE * GELU_CUBIC) * square))
        act_low = (u * half).astype(LOW)
        act[:, span] = act_low
        steep = u * (2.0 * GELU_SLOPE + (6.0 * GELU_SLOPE * GELU_CUBIC) * square)
        slope[:, span] = half + (half - half * half) * steep
        result = result + dot_nt(act_low, wd[:, span])
    result = (result + bias_down[...]).reshape(count, LEN, D)
    gate = mod[:, 5:6, :]
    out[...] = (mixed + gate * result).astype(LOW)
    upstream = cotangent[...].astype(FULL)
    grad_mod[:, 3:4, :] = jnp.sum(upstream * result, axis=1, keepdims=True)
    grad_result = (gate * upstream).reshape(flat, D).astype(LOW)
    sum_down[...] += jnp.sum(grad_result.astype(FULL), axis=0, keepdims=True)
    grad_hidden = jnp.zeros((flat, D), FULL)
    for start in range(0, FF, CHUNK):
        span = slice(start, start + CHUNK)
        grad_u = (dot(grad_result, wd[:, span]) * slope[:, span]).astype(LOW)
        sum_up[:, span] += jnp.sum(grad_u.astype(FULL), axis=0, keepdims=True)
        total_down[:, span] += dot_tn(grad_result, act[:, span])
        total_up[:, span] += dot_tn(hidden, grad_u)
        grad_hidden = grad_hidden + dot_nt(grad_u, wu[:, span])
    grad_hidden = grad_hidden.reshape(count, LEN, D)
    grad_mod[:, 1:2, :] = jnp.sum(grad_hidden, axis=1, keepdims=True)
    grad_mod[:, 2:3, :] = jnp.sum(grad_hidden * normed, axis=1, keepdims=True)
    back = upstream + normalize_back(
        grad_hidden * (1.0 + mod[:, 4:5, :]), normed, inverse_spread
    )
    grad_mixed[...] = back
    grad_mod[:, 0:1, :] = jnp.sum(back * branch_out, axis=1, keepdims=True)

    @pl.when(step == pl.num_programs(0) - 1)
    def _():
        shard, low = ids[0], ids[1]
        for j in range(GROUP):
            span = pl.ds(pl.multiple_of((low ^ j) * rows, rows), rows)
            for s in range(shards):
                d = lax.rem(s - shard + shards, shards)
                lanes = slice(s * width, (s + 1) * width)
                piece = jnp.concatenate([total_up[span, lanes], total_down[span, lanes]], axis=1)
                if j & 1:
                    send[j // 2, d] = piece.astype(LOW)
                else:
                    keep[j // 2, d] = piece


def attention_backward(
    ids, mod, attended, grad_mixed, qkv, probs, wo,
    grad_qkv, total_project,
    grad_attended,
):
    @pl.when(pl.program_id(0) == 0)
    def _():
        total_project[...] = jnp.zeros_like(total_project)

    count = attended.shape[0]
    flat = count * LEN
    grad_branch = (mod[:, 2:3, :] * grad_mixed[...]).reshape(flat, D).astype(LOW)
    total_project[...] += dot_tn(attended[...].reshape(flat, D), grad_branch)
    grad_attended[...] = dot(grad_branch, wo[...]).astype(LOW).reshape(count, LEN, D)
    mask = lax.broadcasted_iota(jnp.int32, (LEN, PAIR), 1) < HEAD
    scale = HEAD ** (-0.5)
    for latent in range(count):
        for pair in range(HEADS // 2):
            lanes = slice(pair * PAIR, (pair + 1) * PAIR)
            key_lanes = slice(D + pair * PAIR, D + (pair + 1) * PAIR)
            value_lanes = slice(2 * D + pair * PAIR, 2 * D + (pair + 1) * PAIR)
            queries = qkv[latent, :, lanes]
            keys = qkv[latent, :, key_lanes].T
            values = qkv[latent, :, value_lanes]
            upper = grad_attended[latent, :, lanes]
            masked = head_masks(upper.astype(FULL))
            by_query, by_key, by_value = [], [], []
            for member in range(2):
                share = probs[latent, 2 * pair + member]
                weight = share.astype(FULL)
                grad_share = dot_nt(values, masked[member])
                product = weight * grad_share
                grad_scores = (
                    product - weight * jnp.sum(product, 0, keepdims=True)
                ).astype(LOW)
                by_query.append(dot(keys[member * HEAD : (member + 1) * HEAD], grad_scores))
                by_key.append(dot(grad_scores, queries))
                by_value.append(dot(share, upper))
            merged = jnp.concatenate(by_query, axis=0).T * scale
            grad_qkv[latent, :, lanes] = merged.astype(LOW)
            merged = jnp.where(mask, by_key[0], by_key[1]) * scale
            grad_qkv[latent, :, key_lanes] = merged.astype(LOW)
            merged = jnp.where(mask, by_value[0], by_value[1])
            grad_qkv[latent, :, value_lanes] = merged.astype(LOW)


def attend_backward(
    ids, tokens, mod, grad_mixed, grad_qkv, wq, total_project, grad_mod_late, sum_up, sum_down,
    grad_tokens, keep, send, extra,
    total_attend, grad_mod, extra_rows,
):
    rows = D // GROUP
    shards = keep.shape[1]
    step = pl.program_id(0)

    @pl.when(step == 0)
    def _():
        total_attend[...] = jnp.zeros_like(total_attend)

    count = tokens.shape[0]
    flat = count * LEN
    normed, inverse_spread = normalize(tokens[...].astype(FULL))
    hidden = (normed * (1.0 + mod[:, 1:2, :]) + mod[:, 0:1, :]).reshape(flat, D).astype(LOW)
    grad_low = grad_qkv[...].reshape(flat, 3 * D)
    total_attend[...] += dot_tn(hidden, grad_low)
    grad_hidden = dot(grad_low, wq[...]).reshape(count, LEN, D)
    mine = pl.ds(step * count, count)
    grad_mod[mine, 0:1, :] = jnp.sum(grad_hidden, axis=1, keepdims=True)
    grad_mod[mine, 1:2, :] = jnp.sum(grad_hidden * normed, axis=1, keepdims=True)
    grad_tokens[...] = grad_mixed[...] + normalize_back(
        grad_hidden * (1.0 + mod[:, 1:2, :]), normed, inverse_spread
    )

    @pl.when(step == pl.num_programs(0) - 1)
    def _():
        shard, low = ids[0], ids[1]
        wide, narrow = 3 * D // shards, D // shards
        for j in range(GROUP):
            span = rows_at(low ^ j, rows)
            whole_attend, whole_project = total_attend[span, :], total_project[span, :]
            for s in range(shards):
                d = lax.rem(s - shard + shards, shards)
                piece = jnp.concatenate(
                    [
                        whole_attend[:, s * wide : (s + 1) * wide],
                        whole_project[:, s * narrow : (s + 1) * narrow],
                    ],
                    axis=1,
                )
                if j & 1:
                    send[j // 2, d] = piece.astype(LOW)
                else:
                    keep[j // 2, d] = piece
        latents = grad_mod.shape[0]
        columns = [grad_mod[:, b, :] for b in range(2)] + [grad_mod_late[:, b, :] for b in range(4)]
        whole = jnp.concatenate(columns, axis=1).astype(LOW).astype(FULL)
        sums = jnp.sum(whole, axis=0, keepdims=True)
        sums = jnp.concatenate([sums, sum_up[...], sum_down[...]], axis=1)
        mod_share, bias_share = 6 * D // shards, BIAS_LEN // shards
        blocks, lines = -(-mod_share // D), -(-bias_share // D)

        def padded(values, start, stop):
            part = values[:, start : min(start + D, stop)]
            if part.shape[1] < D:
                rest = jnp.zeros((part.shape[0], D - part.shape[1]), FULL)
                part = jnp.concatenate([part, rest], axis=1)
            return part

        extra_rows[...] = jnp.zeros_like(extra_rows)
        for s in range(shards):
            for b in range(blocks):
                extra_rows[b * latents : (b + 1) * latents, :] = padded(
                    whole, s * mod_share + b * D, (s + 1) * mod_share
                )
            for b in range(lines):
                row = padded(sums, s * bias_share + b * D, (s + 1) * bias_share)
                high = row.astype(LOW).astype(FULL)
                place = blocks * latents + b
                extra_rows[place : place + 1, :] = high
                extra_rows[place + lines : place + lines + 1, :] = row - high
            extra[lax.rem(s - shard + shards, shards)] = extra_rows[...].astype(LOW)


def late_pieces(ids, own, first, second, third, extra, *pieces):
    total = own[...]
    for received in (first, second, third):
        total = total + received[...].astype(FULL)
    for d, piece in enumerate(pieces):
        piece[:NOTE, :] = extra[d]
        if total.shape[2] < D:
            piece[NOTE:, :] = jnp.zeros((total.shape[1], D), LOW)
        piece[NOTE:, : total.shape[2]] = total[d].astype(LOW)


def combine(shards, latents, ids, *refs):
    incoming, notes, weight, payload = (
        refs[:shards], refs[shards : 2 * shards], refs[2 * shards], refs[2 * shards + 1],
    )
    answers, rows_ref = refs[2 * shards + 2 : -1], refs[-1]
    rows = D // GROUP
    mod_share, bias_share = 6 * D // shards, BIAS_LEN // shards
    blocks, lines = -(-mod_share // D), -(-bias_share // D)
    total = jnp.zeros((rows, D), FULL)
    bias = jnp.zeros((NOTE, D), FULL)
    for d in range(shards):
        total = total + incoming[d][NOTE:, :].astype(FULL)
        extra = incoming[d][:NOTE, :].astype(FULL)
        bias = bias + extra
        for b in range(blocks):
            start = (b * shards + d) * latents
            rows_ref[start : start + latents, :] = extra[b * latents : (b + 1) * latents]
        start = (blocks * shards + d) * latents
        rows_ref[start : start + latents, :] = notes[d][:NOTE, :].astype(FULL)[:latents]
    payload[:rows, :] = total.astype(LOW)
    count = (blocks + 1) * shards * latents
    start = blocks * latents
    bias = bias[start : start + lines] + bias[start + lines : start + 2 * lines]
    high = bias.astype(LOW).astype(FULL)
    rows_ref[count:, :] = jnp.zeros((16, D), FULL)
    rows_ref[count : count + lines, :] = high
    rows_ref[count + 8 : count + 8 + lines, :] = bias - high
    payload[rows:, :] = rows_ref[...].astype(LOW)
    for d, answer in enumerate(answers):
        result = jnp.zeros((NOTE, D), FULL)
        for b in range(blocks):
            filled = min(D, mod_share - b * D)
            product = dot(incoming[d][:NOTE, :filled], weight[b * D : b * D + filled, :])
            result = result + shifted(product, b * latents)
        answer[...] = result[:latents]


def shifted(values, count):
    if count == 0:
        return values
    return jnp.concatenate([values[count:], values[:count]], axis=0)


COLUMNS = (3 * D, D, FF, FF, 6 * D)
TURNED = (True, True, False, False, True)
TRIANGLE = ((0, 0), (0, 1), (0, 2), (1, 1), (1, 2), (2, 2))


def slot_spans(widths):
    counts = [sum(1 for m, _ in SLOTS if m == number) for number in range(len(widths))]
    return [
        (part * (widths[m] // counts[m]), (part + 1) * (widths[m] // counts[m]))
        for m, part in SLOTS
    ]


def late_parts(latents, widths, late, late_flipped):
    rows = D // GROUP
    blocks = -(-widths[4] // D)
    unit = (blocks + 1) * latents + 16
    parts = [
        ref.at[t, pl.ds(start, unit), :]
        for ref in (late, late_flipped)
        for t in range(GROUP // 2)
        for start in range(rows, late.shape[1], unit)
    ]

    def rows_of(start):
        return jnp.concatenate([p[start : start + latents, :] for p in parts], axis=0)

    return parts, blocks, rows_of


def modulate_gradient(latents, widths, late, late_flipped, target):
    _, blocks, rows_of = late_parts(latents, widths, late, late_flipped)
    cond = rows_of(blocks * latents)
    for block in range(blocks):
        filled = min(D, widths[4] - block * D)
        target[block * D : block * D + filled, :] = dot_tn(rows_of(block * latents), cond)[:filled]


def late_gradient(ids, late, late_flipped, late_whole):
    rows = D // GROUP
    for place, block in pieces_of(ids, late, late_flipped):
        late_whole[rows_at(place, rows), :] = block[:rows, :].astype(FULL)
    return turn(late_whole[...])


def mix(moment, grad):
    moment = MOMENTUM * moment + grad
    return moment, grad + MOMENTUM * moment


def gram_kernel(latents, ids, late, late_flipped, early, early_flipped, *refs):
    moments, gram, columns = refs[0:5], refs[5], refs[6]
    late_whole, flat_gram, early_whole, modulate_whole = refs[7:11]
    low = ids[1]
    rows = D // GROUP
    shards = gram.shape[0]
    widths = [whole // shards for whole in COLUMNS]
    spans = slot_spans(widths)
    for number in range(5):
        owners = [k for k, (m, _) in enumerate(SLOTS) if m == number]
        condition = low == owners[0]
        for owner in owners[1:]:
            condition = condition | (low == owner)

        @pl.when(condition)
        def _(number=number, owners=owners):
            if number < 2:
                start = 0 if number == 0 else widths[0]
                grad = late_gradient(ids, late, late_flipped, late_whole)
                grad = grad[start : start + widths[number]]
            elif number < 4:
                start = 0 if number == 2 else widths[2]
                for place, block in pieces_of(ids, early, early_flipped):
                    piece = block[...].astype(FULL)[:, start : start + widths[number]]
                    early_whole[rows_at(place, rows), :] = piece
                grad = early_whole[...]
            else:
                modulate_gradient(latents, widths, late, late_flipped, modulate_whole)
                grad = modulate_whole[...]
            mixed = mix(moments[number][...], grad)[1]
            parts = split_low(mixed)
            whole = dot_split(parts, parts, dot_tn if TURNED[number] else dot_nt)
            for place, (a, b) in enumerate(TRIANGLE):
                flat_gram[place * 128 : (place + 1) * 128, :] = whole[
                    a * 128 : (a + 1) * 128, b * 128 : (b + 1) * 128
                ]
            if not TURNED[number]:
                mixed = turn(mixed)
            for owner in owners:

                @pl.when(low == owner)
                def _(owner=owner, mixed=mixed):
                    start, stop = spans[owner]
                    filled = stop - start
                    columns[:filled, :] = mixed[start:stop]
                    if filled < columns.shape[0]:
                        columns[filled:, :] = jnp.zeros((columns.shape[0] - filled, D), FULL)

    size = gram.shape[1]
    for s in range(shards):
        gram[lax.rem(s - ids[0] + shards, shards)] = flat_gram[s * size : (s + 1) * size, :]


def momenta_kernel(latents, ids, late, late_flipped, early, early_flipped, *refs):
    moments, grads, momenta = refs[0:5], refs[5:10], refs[10:15]
    bias, late_whole = refs[15:17]
    rows = D // GROUP
    widths = [m.shape[0 if turned else 1] for m, turned in zip(moments, TURNED)]
    turned = late_gradient(ids, late, late_flipped, late_whole)
    grads[0][...] = turned[: widths[0]]
    grads[1][...] = turned[widths[0] : widths[0] + widths[1]]
    for place, block in pieces_of(ids, early, early_flipped):
        piece = block[...].astype(FULL)
        grads[2][rows_at(place, rows), :] = piece[:, : widths[2]]
        grads[3][rows_at(place, rows), :] = piece[:, widths[2] :]
    modulate_gradient(latents, widths, late, late_flipped, grads[4])
    parts, blocks, _ = late_parts(latents, widths, late, late_flipped)
    total = jnp.zeros((16, D), FULL)
    for part in parts:
        total = total + part[(blocks + 1) * latents :, :].astype(FULL)
    bias[...] = total[:8] + total[8:]
    for number in range(5):
        momenta[number][...] = mix(moments[number][...], grads[number][...])[0]


def polynomial_kernel(ids, *refs):
    shards = len(refs) - 5
    pieces, columns, answer, flat_gram, gram_ref, product_ref = refs[:shards], *refs[shards:]
    size = pieces[0].shape[0]
    for d in range(shards):
        source = lax.rem(ids[0] - d + shards, shards)
        flat_gram[rows_at(source, size), :] = pieces[d][...]
    for place, (a, b) in enumerate(TRIANGLE):
        block = flat_gram[place * 128 : (place + 1) * 128, :]
        gram_ref[a * 128 : (a + 1) * 128, b * 128 : (b + 1) * 128] = block
        if a != b:
            gram_ref[b * 128 : (b + 1) * 128, a * 128 : (a + 1) * 128] = block.T
    gram = gram_ref[...]
    diagonal = lax.broadcasted_iota(jnp.int32, (D, D), 0) == lax.broadcasted_iota(
        jnp.int32, (D, D), 1
    )
    trace = jnp.sum(jnp.where(diagonal, gram, 0.0))
    scale = 1.0 / (jnp.sqrt(jnp.full((1, 1), trace)) + 1e-07)
    gram = (gram * scale) * scale

    def advance(gram, product):
        mixing = POLY_CUBIC * gram + POLY_QUINTIC * dot(left_deep(gram), right_deep(gram))
        mixing_deep = left_deep(mixing)
        both = jnp.concatenate([gram, product], axis=1)
        both = POLY_LINEAR * both + dot(mixing_deep, right_deep(both))
        half = both[:, :D]
        return POLY_LINEAR * half + dot(mixing_deep, right_deep(half)), both[:, D:]

    gram_ref[...] = gram
    product_ref[...] = jnp.where(diagonal, 1.0, 0.0)

    @pl.loop(0, NS_ITERS - 1)
    def _(step):
        gram, product = advance(gram_ref[...], product_ref[...])
        gram_ref[...] = gram
        product_ref[...] = product

    gram, product = gram_ref[...], product_ref[...]
    mixing = POLY_CUBIC * gram + POLY_QUINTIC * dot(left_deep(gram), right_deep(gram))
    product = POLY_LINEAR * product + dot(left_deep(mixing), right_deep(product))
    answer[...] = dot(left_deep(columns[...] * scale), right_deep(product)).astype(LOW)


def left_deep(value):
    high, rest = split_low(value)
    return jnp.concatenate([high, rest, high], axis=1)


def right_deep(value):
    high, rest = split_low(value)
    return jnp.concatenate([high, high, rest], axis=0)


def update_kernel(ids, answers, answers_flipped, *refs):
    masters, updated, ordered = refs[:5], refs[5:10], refs[10]
    for place, block in pieces_of(ids, answers, answers_flipped):
        ordered[place] = block[...]
    widths = [m.shape[0 if turned else 1] for m, turned in zip(masters, TURNED)]
    spans = slot_spans(widths)
    for number in range(5):
        factor = MUON_RATE * 0.2 * math.sqrt(COLUMNS[number])
        mine = [k for k, (m, _) in enumerate(SLOTS) if m == number]
        if TURNED[number]:
            for k in mine:
                start, stop = spans[k]
                updated[number][start:stop, :] = masters[number][start:stop, :] * (
                    1.0 - MUON_RATE * WEIGHT_DECAY
                ) - factor * ordered[k, : stop - start, :].astype(FULL)
        else:
            direction = jnp.concatenate(
                [ordered[k, : spans[k][1] - spans[k][0], :].astype(FULL) for k in mine], axis=0
            )
            updated[number][...] = masters[number][...] * (
                1.0 - MUON_RATE * WEIGHT_DECAY
            ) - factor * direction.T


def per_device(
    tokens,
    condition,
    cotangent,
    attend_weight,
    project_weight,
    expand_weight,
    contract_weight,
    modulate_weight,
    biases,
    attend_moment,
    project_moment,
    expand_moment,
    contract_moment,
    modulate_moment,
    bias_first,
    bias_second,
):
    latents = tokens.shape[0]
    steps = latents // BLOCK
    shards = lax.axis_size("shard")
    shard = lax.axis_index("shard")
    low = lax.axis_index("rep") % GROUP
    ids = jnp.stack([shard, low]).astype(jnp.int32)
    rows = D // GROUP
    bias_share = biases.shape[0]
    mod_share = modulate_weight.shape[1]
    late_width = 4 * D // shards
    late_rows = late_width // GROUP

    (note,) = local_call(
        prepare,
        ids,
        [
            (condition, False),
            (biases.reshape(1, -1), False),
            (attend_weight.T, (late_rows, lambda place: jnp.minimum(place, 5))),
            (project_weight.T, (late_rows, lambda place: jnp.maximum(place - 6, 0))),
        ],
        [((NOTE + late_rows, D), LOW, False)],
        [pltpu.VMEM((NOTE, D), FULL)],
        1,
        D * D,
        "prepare",
    )
    notes = exchange([note] * shards)

    *shares, modulate_low, late_weights = local_call(
        modulation_kernel,
        ids,
        [(piece, False) for piece in notes] + [(modulate_weight.T, False)],
        [((latents, mod_share), FULL, False)] * shards
        + [((mod_share, D), LOW, False), ((shards, late_rows, D), LOW, False)],
        [],
        1,
        2 * shards * NOTE * D * mod_share,
        "modulation",
    )
    answers = [shares[0]] + [shift(shares[d], shards - d) for d in range(1, shards)]
    late_weights_chips = gather_chips(late_weights)
    (early_weights,) = local_call(
        pack,
        ids,
        [(w, (rows, lambda place: place)) for w in (expand_weight, contract_weight)],
        [((rows, 2 * FF // shards), LOW, False)],
        [],
        1,
        D * D,
        "pack",
        after=(late_weights,),
    )
    early_weights = jnp.stack(exchange([early_weights] * shards))
    early_weights_chips = gather_chips(early_weights)
    (late_stacked,) = local_call(
        stack,
        ids,
        [(v, False) for v in late_weights_chips],
        [((GROUP // 2, shards, late_rows, D), LOW, False)],
        [],
        1,
        D * D,
        "stack_late",
        after=(early_weights,),
    )
    late_flipped = flip(late_stacked, 1)

    tokens_shape = (latents, LEN, D)
    qkv, probs, attended, branch, wq, wo, mod, bias_up, bias_down = local_call(
        attention_forward,
        ids,
        [(tokens, True), (late_stacked, False), (late_flipped, False)]
        + [(v, False) for v in (*answers, *notes)],
        [
            ((latents, LEN, 3 * D), LOW, True),
            ((latents, HEADS, LEN, LEN), LOW, True),
            (tokens_shape, LOW, True),
            (tokens_shape, FULL, True),
            ((3 * D, D), LOW, False),
            ((D, D), LOW, False),
            ((latents, 6, D), FULL, False),
            ((1, FF), FULL, False),
            ((1, D), FULL, False),
        ],
        [
            pltpu.VMEM((shards, late_width, D), LOW if late_rows % 16 == 0 else FULL),
            pltpu.VMEM((BLOCK * LEN, D), LOW),
            pltpu.VMEM((BLOCK * LEN, D), LOW),
            pltpu.VMEM((shards, latents, mod_share), FULL),
            pltpu.VMEM((shards, NOTE, D), FULL),
            pltpu.VMEM((D, 3 * D), LOW),
            pltpu.VMEM((D, D), LOW),
        ],
        steps,
        latents * (2 * LEN * D * 4 * D + 4 * HEADS * LEN * LEN * PAIR) * 2,
        "attention_forward",
        after=(early_weights,),
    )
    early_shape = (GROUP // 2, shards, rows, 2 * FF // shards)
    (early_weights_stacked,) = local_call(
        stack,
        ids,
        [(v, False) for v in early_weights_chips],
        [(early_shape, LOW, False)],
        [],
        1,
        D * D,
        "stack",
        after=(branch,),
    )
    early_weights_flipped = flip(early_weights_stacked, 1)
    block_output, grad_mixed, grad_mod_late, keep, send, sum_up, sum_down = local_call(
        perceptron,
        ids,
        [
            (tokens, True),
            (branch, True),
            (mod, True),
            (cotangent, True),
            (early_weights_stacked, False),
            (early_weights_flipped, False),
            (bias_up, False),
            (bias_down, False),
        ],
        [
            (tokens_shape, LOW, True),
            (tokens_shape, FULL, True),
            ((latents, 4, D), FULL, True),
            (early_shape, FULL, False),
            (early_shape, LOW, False),
            ((1, FF), FULL, False),
            ((1, D), FULL, False),
        ],
        [
            pltpu.VMEM((shards, D, 2 * FF // shards), LOW),
            pltpu.VMEM((D, FF), LOW),
            pltpu.VMEM((D, FF), LOW),
            pltpu.VMEM((BLOCK * LEN, FF), LOW),
            pltpu.VMEM((BLOCK * LEN, FF), FULL),
            pltpu.VMEM((D, FF), FULL),
            pltpu.VMEM((D, FF), FULL),
        ],
        steps,
        latents * 2 * LEN * D * FF * 6 * 2,
        "perceptron",
    )

    early_totals = sum_cores(keep, send, ids, "early_sum", ())
    arrived = exchange_chips(early_totals)
    early_chips = sum(piece.astype(FULL) for piece in arrived[1:]) + arrived[0]
    grad_qkv, total_project = local_call(
        attention_backward,
        ids,
        [
            (mod, True),
            (attended, True),
            (grad_mixed, True),
            (qkv, True),
            (probs, True),
            (wo, False),
        ],
        [((latents, LEN, 3 * D), LOW, True), ((D, D), FULL, False)],
        [pltpu.VMEM((1, LEN, D), LOW)],
        latents,
        latents * (10 * HEADS * LEN * LEN * PAIR + 4 * LEN * D * D),
        "attention_backward",
        after=tuple(early_totals[1:]),
    )
    early_pieces = exchange([early_chips[d].astype(LOW) for d in range(shards)])
    late_shape = (GROUP // 2, shards, rows, late_width)
    tokens_grad, keep, send, extra = local_call(
        attend_backward,
        ids,
        [
            (tokens, True),
            (mod, True),
            (grad_mixed, True),
            (grad_qkv, True),
            (wq, False),
            (total_project, False),
            (grad_mod_late, False),
            (sum_up, False),
            (sum_down, False),
        ],
        [
            (tokens_shape, FULL, True),
            (late_shape, FULL, False),
            (late_shape, LOW, False),
            ((shards, NOTE, D), LOW, False),
        ],
        [
            pltpu.VMEM((D, 3 * D), FULL),
            pltpu.VMEM((latents, 2, D), FULL),
            pltpu.VMEM((NOTE, D), FULL),
        ],
        steps,
        latents * 2 * LEN * D * 6 * D * 2,
        "attend_backward",
        after=(early_chips,),
    )

    late_totals = sum_cores(keep, send, ids, "late_sum", ())
    arrived = exchange_chips(late_totals)
    (early,) = local_call(
        total_kernel,
        ids,
        [(v, False) for v in (early_chips[0], *early_pieces[1:])],
        [(early_pieces[1].shape, LOW, False)],
        [],
        1,
        D * D,
        "early_total",
        after=tuple(late_totals[1:]),
    )
    early_stacked, early_flipped = gather_group(sum_rest(early))
    outgoing = local_call(
        late_pieces,
        ids,
        [(v, False) for v in (*arrived, extra)],
        [((NOTE + rows, D), LOW, False)] * shards,
        [],
        1,
        4 * shards * rows * late_width,
        "late_pieces",
        after=(early,),
    )
    group_latents = shards * latents
    unit = (-(-mod_share // D) + 1) * group_latents + 16
    payload, *shares = local_call(
        partial(combine, shards, latents),
        ids,
        [(v, False) for v in (*exchange(outgoing), *notes, modulate_low)],
        [((rows + unit, D), LOW, False)] + [((latents, D), FULL, False)] * shards,
        [pltpu.VMEM((unit, D), FULL)],
        1,
        2 * shards * NOTE * D * mod_share,
        "combine",
        after=(early_stacked,),
    )
    if lax.axis_size("rep") > GROUP:
        late, others = sum_rest(payload[:rows]), payload[rows:]
        for bit in range(3, lax.axis_size("rep").bit_length() - 1):
            others = jnp.concatenate([others, flip(others, 1 << bit)], axis=0)
        payload = jnp.concatenate([late, others], axis=0)
    late_stacked, late_flipped = gather_group(payload)

    grad_cond_low = shares[0]
    for d in range(1, shards):
        grad_cond_low = grad_cond_low + shift(shares[d], shards - d)
    _, silu_back = jax.vjp(jax.nn.silu, condition.astype(FULL))
    condition_grad = silu_back(grad_cond_low)[0]

    def as_held(values):
        return [v.T if turned else v for v, turned in zip(values, TURNED)]

    masters = as_held(
        [attend_weight, project_weight, expand_weight, contract_weight, modulate_weight]
    )
    moments = as_held(
        [attend_moment, project_moment, expand_moment, contract_moment, modulate_moment]
    )
    shapes = [m.shape for m in masters]
    widths = [whole // shards for whole in COLUMNS]
    slot_width = max(stop - start for start, stop in slot_spans(widths))
    piece_rows = 128 * len(TRIANGLE) // shards
    sources = [
        (v, False) for v in (late_stacked, late_flipped, early_stacked, early_flipped, *moments)
    ]
    gram, columns = local_call(
        partial(gram_kernel, group_latents),
        ids,
        sources,
        [((shards, piece_rows, 128), FULL, False), ((slot_width, D), FULL, False)],
        [
            pltpu.VMEM((D, D), FULL),
            pltpu.VMEM((128 * len(TRIANGLE), 128), FULL),
            pltpu.VMEM(shapes[2], FULL),
            pltpu.VMEM(shapes[4], FULL),
        ],
        1,
        6 * D * D * D,
        "gram",
    )
    *results, bias_block = local_call(
        partial(momenta_kernel, group_latents),
        ids,
        sources,
        [(shape, FULL, False) for shape in shapes * 2] + [((8, D), FULL, False)],
        [pltpu.VMEM((D, D), FULL)],
        1,
        D * D * D,
        "momenta",
        after=(gram,),
    )
    gradients, momenta = as_held(results[0:5]), as_held(results[5:10])
    piece = sum(exchange([gram[d] for d in range(shards)]))
    (answer,) = local_call(
        polynomial_kernel,
        ids,
        [(p, False) for p in exchange([piece] * shards)] + [(columns, False)],
        [((slot_width, D), LOW, False)],
        [
            pltpu.VMEM((128 * len(TRIANGLE), 128), FULL),
            pltpu.VMEM((D, D), FULL),
            pltpu.VMEM((D, D), FULL),
        ],
        1,
        2 * 3 * 18 * D * D * D,
        "polynomial",
        after=(condition_grad, bias_block),
    )
    updated = local_call(
        update_kernel,
        ids,
        [(v, False) for v in (*gather_group(answer), *masters)],
        [(shape, FULL, False) for shape in shapes],
        [pltpu.VMEM((GROUP, slot_width, D), LOW)],
        1,
        2 * D * sum(widths),
        "update",
    )
    updated = as_held(updated)

    bias_gradient = bias_block.reshape(-1)[:bias_share]
    bias_momentum = BETA_ONE * bias_first + (1.0 - BETA_ONE) * bias_gradient
    bias_variance = BETA_TWO * bias_second + (1.0 - BETA_TWO) * bias_gradient * bias_gradient
    corrected_first = bias_momentum / (1.0 - BETA_ONE**STEP)
    corrected_second = bias_variance / (1.0 - BETA_TWO**STEP)
    bias_updated = biases * (1.0 - ADAM_RATE * WEIGHT_DECAY) - ADAM_RATE * corrected_first / (
        jnp.sqrt(corrected_second) + ADAM_EPSILON
    )
    return (
        block_output,
        tokens_grad,
        condition_grad,
        *gradients,
        *momenta,
        *updated,
        bias_gradient,
        bias_momentum,
        bias_variance,
        bias_updated,
    )


def solution(mesh):
    rows = P(("shard", "rep"), None, None)
    vectors = P(("shard", "rep"), None)
    columns = P(None, "shard")
    flat = P("shard")
    return jax.shard_map(
        per_device,
        mesh=mesh,
        in_specs=(rows, vectors, rows) + (columns,) * 5 + (flat,) + (columns,) * 5 + (flat,) * 2,
        out_specs=(rows, rows, vectors) + (columns,) * 15 + (flat,) * 4,
        check_vma=False,
    )
```

profile of v0, /device:TPU:0, one launch (start us, length us, event | category | flops | bytes accessed | tf_op | source)
XLA Modules:
  0.0 187.2 jit_solution(1605119480791162416)
XLA Ops:
  4.7 5.1 %collective-permute-start.2 = (bf16[64,384]{1,0:T(8,128)(2,1)S(1)}, bf16[64,384]{1,0:T(8,128)(2,1)S(1)}, u32[]{:S(2)}, u32[]{:S(2)}) collective-permute-start(bf16[64,384]{1,0:T(8,128)(2,1)S(1)} %prepare.1.refs_1_.refs_8_.refs_5_), channel_id=1, source_target_pairs={{0,24},{8,0},{16,8},{24,16},{1,25},{9,1},{17,9},{25,17},{2,26},{10... | collective-permute-start | bytes 147464 | tf_op jit(solution)/shard_map/ppermute | solution.py:56
  11.9 2.9 %collective-permute-done.1.refs_3_.refs_10_.refs_7_ = bf16[64,384]{1,0:T(8,128)(2,1)S(1)} collective-permute-done((bf16[64,384]{1,0:T(8,128)(2,1)S(1)}, bf16[64,384]{1,0:T(8,128)(2,1)S(1)}, u32[]{:S(2)}, u32[]{:S(2)}) %collective-permute-start.1) | collective-permute-done | bytes 49184 | tf_op jit(solution)/shard_map/ppermute | solution.py:56
  22.9 2.4 %collective-permute-start.5 = (bf16[4,48,384]{2,1,0:T(8,128)(2,1)S(1)}, bf16[4,48,384]{2,1,0:T(8,128)(2,1)S(1)}, u32[]{:S(2)}, u32[]{:S(2)}) collective-permute-start(bf16[4,48,384]{2,1,0:T(8,128)(2,1)S(1)} %get-tuple-element.85.refs_3_.refs_1_), channel_id=1, source_target_pairs={{0,6},{1,7},{2,4},{3,5},{4,2},{5,3},{6,0},{7,1},{8,14},{9,15},{10,... | collective-permute-start | bytes 442376 | tf_op jit(solution)/shard_map/ppermute | solution.py:61
  28.0 2.5 %collective-permute-done.5.refs_4_ = bf16[4,48,384]{2,1,0:T(8,128)(2,1)S(1)} collective-permute-done((bf16[4,48,384]{2,1,0:T(8,128)(2,1)S(1)}, bf16[4,48,384]{2,1,0:T(8,128)(2,1)S(1)}, u32[]{:S(2)}, u32[]{:S(2)}) %collective-permute-start.5) | collective-permute-done | bytes 147488 | tf_op jit(solution)/shard_map/ppermute | solution.py:61
  31.9 2.1 %collective-permute-start.10 = (f32[4,576]{1,0:T(4,128)S(1)}, f32[4,576]{1,0:T(4,128)S(1)}, u32[]{:S(2)}, u32[]{:S(2)}) collective-permute-start(f32[4,576]{1,0:T(4,128)S(1)} %get-tuple-element.87), channel_id=1, source_target_pairs={{0,24},{8,0},{16,8},{24,16},{1,25},{9,1},{17,9},{25,17},{2,26},{10... | collective-permute-start | bytes 27656 | tf_op jit(solution)/shard_map/ppermute | solution.py:56
  40.3 13.0 %attention_forward.1 = (bf16[4,256,1152]{2,1,0:T(8,128)(2,1)S(1)}, bf16[4,6,256,256]{3,2,1,0:T(8,128)(2,1)S(1)}, bf16[4,256,384]{2,1,0:T(8,128)(2,1)S(1)}, f32[4...) custom-call(s32[2]{0:T(128)S(1)} %pad_add_fusion.refs_0_, ...), custom_call_target="tpu_custom_call" | custom-call | flops 4026531840 | bytes 11288064 | tf_op jit(solution)/shard_map/attention_forward/pallas_call | solution.py:156
  54.0 2.8 %collective-permute-done.16.refs_6_ = bf16[4,4,48,768]{3,2,1,0:T(8,128)(2,1)S(1)} collective-permute-done((bf16[4,4,48,768]{3,2,1,0:T(8,128)(2,1)S(1)}, bf16[4,4,48,768]{3,2,1,0:T(8,128)(2,1)S(1)}, u32[]{:S(2)}, u32[]{:S(2)}) %collective-permute-start.16) | collective-permute-done | bytes 1179680 | tf_op jit(solution)/shard_map/ppermute | solution.py:61
  56.8 14.0 %perceptron.1 = (bf16[4,256,384]{2,1,0:T(8,128)(2,1)}, f32[4,256,384]{2,1,0:T(8,128)S(1)}, f32[4,4,384]{2,1,0:T(4,128)S(1)}, f32[4,4,48,768]{3,2,1,0:T(8,128)S(1...) custom-call(s32[2]{0:T(128)S(1)} %pad_add_fusion.refs_0_, ...), custom_call_target="tpu_custom_call" | custom-call | flops 14495514624 | bytes 11480064 | tf_op jit(solution)/shard_map/perceptron/pallas_call | solution.py:156
  70.9 2.7 %collective-permute-done.17.refs_2_ = bf16[4,4,48,768]{3,2,1,0:T(8,128)(2,1)S(1)} collective-permute-done((bf16[4,4,48,768]{3,2,1,0:T(8,128)(2,1)S(1)}, bf16[4,4,48,768]{3,2,1,0:T(8,128)(2,1)S(1)}, u32[]{:S(2)}, u32[]{:S(2)}) %collective-permute-start.17) | collective-permute-done | bytes 1179680 | tf_op jit(solution)/shard_map/ppermute | solution.py:61
  78.0 10.6 %attention_backward.1 = (bf16[4,256,1152]{2,1,0:T(8,128)(2,1)S(1)}, f32[384,384]{1,0:T(8,128)S(1)}) custom-call(s32[2]{0:T(128)S(1)} %pad_add_fusion.refs_0_, f32[4,6,384]{2,1,0:T(8,128)S(1)} %get-tuple-element.91.refs_3_.refs_1_.refs_2_, bf16[4,256,384]{2,1,0:T(8,128)(2,1)S(1)} %get-tuple-element.96.refs_2_, f32[4,256,384]{2,1,0:T(8,128)S(1)} %get-tuple-element.95.refs_3_, ...), custom_call_target="tpu_custom_call" | custom-call | flops 2617245696 | bytes 11145216 | tf_op jit(solution)/shard_map/attention_backward/pallas_call | solution.py:156
  90.9 6.3 %attend_backward.1 = (f32[4,256,384]{2,1,0:T(8,128)}, f32[4,4,48,384]{3,2,1,0:T(8,128)S(1)}, bf16[4,4,48,384]{3,2,1,0:T(8,128)(2,1)S(1)}, bf16[4,16,384]{2,1,0:T(8,128)(2,1)S(1)}) custom-call(s32[2]{0:T(128)S(1)} %pad_add_fusion.refs_0_, bf16[4,256,384]{2,1,0:T(8,128)(2,1)S(1)} %copy-done.18, f32[4,6,384]{2,1,0:T(8,128)S(1)} %get-tuple-element.91.refs_3_.refs_1_.refs_2_, ...), custom_call_target="tpu_custom_call" | custom-call | flops 3623878656 | bytes 9653760 | tf_op jit(solution)/shard_map/attend_backward/pallas_call | solution.py:156
  97.2 1.9 %collective-permute-start.27 = (bf16[48,768]{1,0:T(8,128)(2,1)S(1)}, bf16[48,768]{1,0:T(8,128)(2,1)S(1)}, u32[]{:S(2)}, u32[]{:S(2)}) collective-permute-start(bf16[48,768]{1,0:T(8,128)(2,1)S(1)} %get-tuple-element.157), channel_id=1, source_target_pairs={{0,24},{8,0},{16,8},{24,16},{1,25},{9,1},{17,9},{25,17},{2,26},{10... | collective-permute-start | bytes 221192 | tf_op jit(solution)/shard_map/ppermute | solution.py:56
  104.3 3.0 %collective-permute-done.26.refs_3_ = bf16[48,768]{1,0:T(8,128)(2,1)S(1)} collective-permute-done((bf16[48,768]{1,0:T(8,128)(2,1)S(1)}, bf16[48,768]{1,0:T(8,128)(2,1)S(1)}, u32[]{:S(2)}, u32[]{:S(2)}) %collective-permute-start.26) | collective-permute-done | bytes 73760 | tf_op jit(solution)/shard_map/ppermute | solution.py:56
  112.1 2.1 %collective-permute-start.28 = (bf16[64,384]{1,0:T(8,128)(2,1)S(1)}, bf16[64,384]{1,0:T(8,128)(2,1)S(1)}, u32[]{:S(2)}, u32[]{:S(2)}) collective-permute-start(bf16[64,384]{1,0:T(8,128)(2,1)S(1)} %get-tuple-element.121), channel_id=1, source_target_pairs={{0,8},{8,16},{16,24},{24,0},{1,9},{9,17},{17,25},{25,1},{2,10},{10... | collective-permute-start | bytes 147464 | tf_op jit(solution)/shard_map/ppermute | solution.py:56
  120.9 2.6 %collective-permute-start.39 = (bf16[112,384]{1,0:T(8,128)(2,1)S(1)}, bf16[112,384]{1,0:T(8,128)(2,1)S(1)}, u32[]{:S(2)}, u32[]{:S(2)}) collective-permute-start(bf16[112,384]{1,0:T(8,128)(2,1)S(1)} %get-tuple-element.129), channel_id=1, source_target_pairs={{0,6},{1,7},{2,4},{3,5},{4,2},{5,3},{6,0},{7,1},{8,14},{9,15},{10,... | collective-permute-start | bytes 258056 | tf_op jit(solution)/shard_map/ppermute | solution.py:61
  130.5 2.0 %gram.1 = (f32[4,192,128]{2,1,0:T(8,128)S(1)}, f32[288,384]{1,0:T(8,128)S(1)}) custom-call(s32[2]{0:T(128)S(1)} %pad_add_fusion.refs_0_, bf16[4,112,384]{2,1,0:T(8,128)(2,1)S(1)} %pad_maximum_fusion.1.refs_1_, bf16[4,112,384]{2,1,0:T(8,128)(2,1)S(1)} %collective-permute-done.40.refs_2_, bf16[4,48,768]{2,1,0:T(8,128)(2,1)S(1)} %pad_maximum_fusion.3.refs_10_.refs_3_, ...), custom_call_target="tpu_custom_call" | custom-call | flops 339738624 | bytes 4767744 | tf_op jit(solution)/shard_map/gram/pallas_call | solution.py:156
  133.1 3.3 %collective-permute-start.44 = (f32[192,128]{1,0:T(8,128)S(1)}, f32[192,128]{1,0:T(8,128)S(1)}, u32[]{:S(2)}, u32[]{:S(2)}) collective-permute-start(f32[192,128]{1,0:T(8,128)S(1)} %get-tuple-element.155), channel_id=1, source_target_pairs={{0,24},{8,0},{16,8},{24,16},{1,25},{9,1},{17,9},{25,17},{2,26},{10... | collective-permute-start | bytes 294920 | tf_op jit(solution)/shard_map/ppermute | solution.py:56
  141.3 4.0 %collective-permute-done.43 = f32[192,128]{1,0:T(8,128)S(1)} collective-permute-done((f32[192,128]{1,0:T(8,128)S(1)}, f32[192,128]{1,0:T(8,128)S(1)}, u32[]{:S(2)}, u32[]{:S(2)}) %collective-permute-start.43) | collective-permute-done | bytes 98336 | tf_op jit(solution)/shard_map/ppermute | solution.py:56
  147.9 3.4 %momenta.1 = (f32[288,384]{1,0:T(8,128)}, f32[96,384]{1,0:T(8,128)}, f32[384,384]{1,0:T(8,128)}, f32[384,384]{1,0:T(8,128)}, f32[576,384]{1,0:T(8,128)}, /*index...) custom-call(s32[2]{0:T(128)S(1)} %pad_add_fusion.refs_0_, ...), custom_call_target="tpu_custom_call" | custom-call | flops 56623104 | bytes 9252864 | tf_op jit(solution)/shard_map/momenta/pallas_call | solution.py:156
  151.3 4.8 %collective-permute-done.46.refs_3_ = f32[192,128]{1,0:T(8,128)S(1)} collective-permute-done((f32[192,128]{1,0:T(8,128)S(1)}, f32[192,128]{1,0:T(8,128)S(1)}, u32[]{:S(2)}, u32[]{:S(2)}) %collective-permute-start.46) | collective-permute-done | bytes 98336 | tf_op jit(solution)/shard_map/ppermute | solution.py:56
  156.1 11.7 %polynomial.1 = bf16[288,384]{1,0:T(8,128)(2,1)S(1)} custom-call(s32[2]{0:T(128)S(1)} %pad_add_fusion.refs_0_, f32[192,128]{1,0:T(8,128)S(1)} %fusion.1.refs_1_, f32[192,128]{1,0:T(8,128)S(1)} %collective-permute-done.45.refs_2_, f32[192,128]{1,0:T(8,128)S(1)} %collective-permute-done.46.refs_3_, f32[192,128]{1,0:T(8,128)S(1)} %collective-permute-done.47.refs_4_, ...), custom_call_target="tpu_custom_call" | custom-call | flops 6115295232 | bytes 1056768 | tf_op jit(solution)/shard_map/polynomial/pallas_call | solution.py:156
  171.4 5.8 %collective-permute-done.50 = bf16[288,384]{1,0:T(8,128)(2,1)S(1)} collective-permute-done((bf16[288,384]{1,0:T(8,128)(2,1)S(1)}, bf16[288,384]{1,0:T(8,128)(2,1)S(1)}, u32[]{:S(2)}, u32[]{:S(2)}) %collective-permute-start.50) | collective-permute-done | bytes 221216 | tf_op jit(solution)/shard_map/ppermute | solution.py:61
  177.2 3.7 %collective-permute-done.49 = bf16[288,384]{1,0:T(8,128)(2,1)S(1)} collective-permute-done((bf16[288,384]{1,0:T(8,128)(2,1)S(1)}, bf16[288,384]{1,0:T(8,128)(2,1)S(1)}, u32[]{:S(2)}, u32[]{:S(2)}) %collective-permute-start.49) | collective-permute-done | bytes 221216 | tf_op jit(solution)/shard_map/ppermute | solution.py:61
  183.6 3.6 %update.1 = (f32[288,384]{1,0:T(8,128)}, f32[96,384]{1,0:T(8,128)}, f32[384,384]{1,0:T(8,128)}, f32[384,384]{1,0:T(8,128)}, f32[576,384]{1,0:T(8,128)}) custom-call(s32[2]{0:T(128)S(1)} %pad_add_fusion.refs_0_, bf16[4,288,384]{2,1,0:T(8,128)(2,1)S(1)} %pad_maximum_fusion.refs_1_, bf16[4,288,384]{2,1,0:T(8,128)(2,1)} %collective-permute-done.51.refs_2_, ...), custom_call_target="tpu_custom_call" | custom-call | flops 1327104 | bytes 7077888 | tf_op jit(solution)/shard_map/update/pallas_call | solution.py:156
  (150 shorter events, 69.9 us)
Async XLA Ops:
  22.9 7.7 %collective-permute-start.5 = (bf16[4,48,384]{2,1,0:T(8,128)(2,1)S(1)}, bf16[4,48,384]{2,1,0:T(8,128)(2,1)S(1)}, u32[]{:S(2)}, u32[]{:S(2)}) collective-permute-start(bf16[4,48,384]{2,1,0:T(8,128)(2,1)S(1)} %get-tuple-element.85.refs_3_.refs_1_), channel_id=1, source_target_pairs={{0,6},{1,7},{2,4},{3,5},{4,2},{5,3},{6,0},{7,1},{8,14},{9,15},{10,... | collective-permute-start | bytes 442376 | tf_op jit(solution)/shard_map/ppermute | solution.py:61
  31.9 8.4 %collective-permute-start.9 = (bf16[4,4,48,384]{3,2,1,0:T(8,128)(2,1)S(1)}, bf16[4,4,48,384]{3,2,1,0:T(8,128)(2,1)S(1)}, u32[]{:S(2)}, u32[]{:S(2)}) collective-permute-start(bf16[4,4,48,384]{3,2,1,0:T(8,128)(2,1)S(1)} %stack_late.1.refs_2_), channel_id=1, source_target_pairs={{0,1},{1,0},{2,3},{3,2},{4,5},{5,4},{6,7},{7,6},{8,9},{9,8},{10,11... | collective-permute-start | bytes 1769480 | tf_op jit(solution)/shard_map/ppermute | solution.py:61
  35.7 17.6 %collective-permute-start.15 = (bf16[4,48,768]{2,1,0:T(8,128)(2,1)S(1)}, bf16[4,48,768]{2,1,0:T(8,128)(2,1)S(1)}, u32[]{:S(2)}, u32[]{:S(2)}) collective-permute-start(bf16[4,48,768]{2,1,0:T(8,128)(2,1)S(1)} %pad_maximum_fusion.2.refs_5_.refs_12_.refs_1_), channel_id=1, source_target_pairs={{0,6},{1,7},{2,4},{3,5},{4,2},{5,3},{6,0},{7,1},{8,14},{9,15},{10,... | collective-permute-start | bytes 884744 | tf_op jit(solution)/shard_map/ppermute | solution.py:61
  37.1 16.2 %collective-permute-start.14 = (bf16[4,48,768]{2,1,0:T(8,128)(2,1)S(1)}, bf16[4,48,768]{2,1,0:T(8,128)(2,1)S(1)}, u32[]{:S(2)}, u32[]{:S(2)}) collective-permute-start(bf16[4,48,768]{2,1,0:T(8,128)(2,1)S(1)} %pad_maximum_fusion.2.refs_5_.refs_12_.refs_1_), channel_id=1, source_target_pairs={{0,4},{1,5},{2,6},{3,7},{4,0},{5,1},{6,2},{7,3},{8,12},{9,13},{10,... | collective-permute-start | bytes 884744 | tf_op jit(solution)/shard_map/ppermute | solution.py:61
  38.6 14.6 %collective-permute-start.13 = (bf16[4,48,768]{2,1,0:T(8,128)(2,1)S(1)}, bf16[4,48,768]{2,1,0:T(8,128)(2,1)S(1)}, u32[]{:S(2)}, u32[]{:S(2)}) collective-permute-start(bf16[4,48,768]{2,1,0:T(8,128)(2,1)S(1)} %pad_maximum_fusion.2.refs_5_.refs_12_.refs_1_), channel_id=1, source_target_pairs={{0,2},{1,3},{2,0},{3,1},{4,6},{5,7},{6,4},{7,5},{8,10},{9,11},{10,... | collective-permute-start | bytes 884744 | tf_op jit(solution)/shard_map/ppermute | solution.py:61
  74.4 14.1 %collective-permute-start.18 = (bf16[4,48,768]{2,1,0:T(8,128)(2,1)S(1)}, bf16[4,48,768]{2,1,0:T(8,128)(2,1)S(1)}, u32[]{:S(2)}, u32[]{:S(2)}) collective-permute-start(bf16[4,48,768]{2,1,0:T(8,128)(2,1)S(1)} %get-tuple-element.102.refs_7_), channel_id=1, source_target_pairs={{0,2},{1,3},{2,0},{3,1},{4,6},{5,7},{6,4},{7,5},{8,10},{9,11},{10,... | collective-permute-start | bytes 884744 | tf_op jit(solution)/shard_map/ppermute | solution.py:61
  75.5 13.7 %collective-permute-start.19 = (bf16[4,48,768]{2,1,0:T(8,128)(2,1)S(1)}, bf16[4,48,768]{2,1,0:T(8,128)(2,1)S(1)}, u32[]{:S(2)}, u32[]{:S(2)}) collective-permute-start(bf16[4,48,768]{2,1,0:T(8,128)(2,1)S(1)} %get-tuple-element.103.refs_8_), channel_id=1, source_target_pairs={{0,4},{1,5},{2,6},{3,7},{4,0},{5,1},{6,2},{7,3},{8,12},{9,13},{10,... | collective-permute-start | bytes 884744 | tf_op jit(solution)/shard_map/ppermute | solution.py:61
  76.5 14.2 %collective-permute-start.20 = (bf16[4,48,768]{2,1,0:T(8,128)(2,1)S(1)}, bf16[4,48,768]{2,1,0:T(8,128)(2,1)S(1)}, u32[]{:S(2)}, u32[]{:S(2)}) collective-permute-start(bf16[4,48,768]{2,1,0:T(8,128)(2,1)S(1)} %get-tuple-element.104.refs_9_), channel_id=1, source_target_pairs={{0,6},{1,7},{2,4},{3,5},{4,2},{5,3},{6,0},{7,1},{8,14},{9,15},{10,... | collective-permute-start | bytes 884744 | tf_op jit(solution)/shard_map/ppermute | solution.py:61
  99.1 8.1 %collective-permute-start.26 = (bf16[48,768]{1,0:T(8,128)(2,1)S(1)}, bf16[48,768]{1,0:T(8,128)(2,1)S(1)}, u32[]{:S(2)}, u32[]{:S(2)}) collective-permute-start(bf16[48,768]{1,0:T(8,128)(2,1)S(1)} %get-tuple-element.158), channel_id=1, source_target_pairs={{0,16},{8,24},{16,0},{24,8},{1,17},{9,25},{17,1},{25,9},{2,18},{10... | collective-permute-start | bytes 221192 | tf_op jit(solution)/shard_map/ppermute | solution.py:56
  100.7 9.5 %collective-permute-start.22 = (bf16[4,48,384]{2,1,0:T(8,128)(2,1)S(1)}, bf16[4,48,384]{2,1,0:T(8,128)(2,1)S(1)}, u32[]{:S(2)}, u32[]{:S(2)}) collective-permute-start(bf16[4,48,384]{2,1,0:T(8,128)(2,1)S(1)} %get-tuple-element.116.refs_5_), channel_id=1, source_target_pairs={{0,2},{1,3},{2,0},{3,1},{4,6},{5,7},{6,4},{7,5},{8,10},{9,11},{10,... | collective-permute-start | bytes 442376 | tf_op jit(solution)/shard_map/ppermute | solution.py:61
  101.4 10.0 %collective-permute-start.23 = (bf16[4,48,384]{2,1,0:T(8,128)(2,1)S(1)}, bf16[4,48,384]{2,1,0:T(8,128)(2,1)S(1)}, u32[]{:S(2)}, u32[]{:S(2)}) collective-permute-start(bf16[4,48,384]{2,1,0:T(8,128)(2,1)S(1)} %get-tuple-element.117.refs_6_), channel_id=1, source_target_pairs={{0,4},{1,5},{2,6},{3,7},{4,0},{5,1},{6,2},{7,3},{8,12},{9,13},{10,... | collective-permute-start | bytes 442376 | tf_op jit(solution)/shard_map/ppermute | solution.py:61
  102.8 8.6 %collective-permute-start.24 = (bf16[4,48,384]{2,1,0:T(8,128)(2,1)S(1)}, bf16[4,48,384]{2,1,0:T(8,128)(2,1)S(1)}, u32[]{:S(2)}, u32[]{:S(2)}) collective-permute-start(bf16[4,48,384]{2,1,0:T(8,128)(2,1)S(1)} %get-tuple-element.118.refs_7_), channel_id=1, source_target_pairs={{0,6},{1,7},{2,4},{3,5},{4,2},{5,3},{6,0},{7,1},{8,14},{9,15},{10,... | collective-permute-start | bytes 442376 | tf_op jit(solution)/shard_map/ppermute | solution.py:61
  107.8 8.1 %collective-permute-start.33 = (bf16[48,768]{1,0:T(8,128)(2,1)S(1)}, bf16[48,768]{1,0:T(8,128)(2,1)S(1)}, u32[]{:S(2)}, u32[]{:S(2)}) collective-permute-start(bf16[48,768]{1,0:T(8,128)(2,1)S(1)} %early_total.1.refs_6_), channel_id=1, source_target_pairs={{0,6},{1,7},{2,4},{3,5},{4,2},{5,3},{6,0},{7,1},{8,14},{9,15},{10,... | collective-permute-start | bytes 221192 | tf_op jit(solution)/shard_map/ppermute | solution.py:61
  132.5 7.5 %collective-permute-start.42 = (f32[192,128]{1,0:T(8,128)S(1)}, f32[192,128]{1,0:T(8,128)S(1)}, u32[]{:S(2)}, u32[]{:S(2)}) collective-permute-start(f32[192,128]{1,0:T(8,128)S(1)} %get-tuple-element.154), channel_id=1, source_target_pairs={{0,8},{8,16},{16,24},{24,0},{1,9},{9,17},{17,25},{25,1},{2,10},{10... | collective-permute-start | bytes 294920 | tf_op jit(solution)/shard_map/ppermute | solution.py:56
  133.1 8.2 %collective-permute-start.44 = (f32[192,128]{1,0:T(8,128)S(1)}, f32[192,128]{1,0:T(8,128)S(1)}, u32[]{:S(2)}, u32[]{:S(2)}) collective-permute-start(f32[192,128]{1,0:T(8,128)S(1)} %get-tuple-element.155), channel_id=1, source_target_pairs={{0,24},{8,0},{16,8},{24,16},{1,25},{9,1},{17,9},{25,17},{2,26},{10... | collective-permute-start | bytes 294920 | tf_op jit(solution)/shard_map/ppermute | solution.py:56
  136.4 9.0 %collective-permute-start.43 = (f32[192,128]{1,0:T(8,128)S(1)}, f32[192,128]{1,0:T(8,128)S(1)}, u32[]{:S(2)}, u32[]{:S(2)}) collective-permute-start(f32[192,128]{1,0:T(8,128)S(1)} %get-tuple-element.156), channel_id=1, source_target_pairs={{0,16},{8,24},{16,0},{24,8},{1,17},{9,25},{17,1},{25,9},{2,18},{10... | collective-permute-start | bytes 294920 | tf_op jit(solution)/shard_map/ppermute | solution.py:56
  136.4 10.9 %collective-permute-start.34 = (f32[4,384]{1,0:T(4,128)S(1)}, f32[4,384]{1,0:T(4,128)S(1)}, u32[]{:S(2)}, u32[]{:S(2)}) collective-permute-start(f32[4,384]{1,0:T(4,128)S(1)} %get-tuple-element.126), channel_id=1, source_target_pairs={{0,24},{8,0},{16,8},{24,16},{1,25},{9,1},{17,9},{25,17},{2,26},{10... | collective-permute-start | bytes 18440 | tf_op jit(solution)/shard_map/ppermute | solution.py:56
  137.5 10.4 %collective-permute-start.35 = (f32[4,384]{1,0:T(4,128)S(1)}, f32[4,384]{1,0:T(4,128)S(1)}, u32[]{:S(2)}, u32[]{:S(2)}) collective-permute-start(f32[4,384]{1,0:T(4,128)S(1)} %get-tuple-element.127), channel_id=1, source_target_pairs={{0,16},{8,24},{16,0},{24,8},{1,17},{9,25},{17,1},{25,9},{2,18},{10... | collective-permute-start | bytes 18440 | tf_op jit(solution)/shard_map/ppermute | solution.py:56
  140.0 7.9 %collective-permute-start.36 = (f32[4,384]{1,0:T(4,128)S(1)}, f32[4,384]{1,0:T(4,128)S(1)}, u32[]{:S(2)}, u32[]{:S(2)}) collective-permute-start(f32[4,384]{1,0:T(4,128)S(1)} %get-tuple-element.128), channel_id=1, source_target_pairs={{0,8},{8,16},{16,24},{24,0},{1,9},{9,17},{17,25},{25,1},{2,10},{10... | collective-permute-start | bytes 18440 | tf_op jit(solution)/shard_map/ppermute | solution.py:56
  147.2 8.9 %collective-permute-start.46 = (f32[192,128]{1,0:T(8,128)S(1)}, f32[192,128]{1,0:T(8,128)S(1)}, u32[]{:S(2)}, u32[]{:S(2)}) collective-permute-start(f32[192,128]{1,0:T(8,128)S(1)} %fusion.1.refs_1_), channel_id=1, source_target_pairs={{0,16},{8,24},{16,0},{24,8},{1,17},{9,25},{17,1},{25,9},{2,18},{10... | collective-permute-start | bytes 294920 | tf_op jit(solution)/shard_map/ppermute | solution.py:56
  147.2 8.9 %collective-permute-start.45 = (f32[192,128]{1,0:T(8,128)S(1)}, f32[192,128]{1,0:T(8,128)S(1)}, u32[]{:S(2)}, u32[]{:S(2)}) collective-permute-start(f32[192,128]{1,0:T(8,128)S(1)} %fusion.1.refs_1_), channel_id=1, source_target_pairs={{0,8},{8,16},{16,24},{24,0},{1,9},{9,17},{17,25},{25,1},{2,10},{10... | collective-permute-start | bytes 294920 | tf_op jit(solution)/shard_map/ppermute | solution.py:56
  167.9 9.3 %collective-permute-start.50 = (bf16[288,384]{1,0:T(8,128)(2,1)S(1)}, bf16[288,384]{1,0:T(8,128)(2,1)S(1)}, u32[]{:S(2)}, u32[]{:S(2)}) collective-permute-start(bf16[288,384]{1,0:T(8,128)(2,1)S(1)} %polynomial.1), channel_id=1, source_target_pairs={{0,6},{1,7},{2,4},{3,5},{4,2},{5,3},{6,0},{7,1},{8,14},{9,15},{10,... | collective-permute-start | bytes 663560 | tf_op jit(solution)/shard_map/ppermute | solution.py:61
  169.6 11.2 %collective-permute-start.49 = (bf16[288,384]{1,0:T(8,128)(2,1)S(1)}, bf16[288,384]{1,0:T(8,128)(2,1)S(1)}, u32[]{:S(2)}, u32[]{:S(2)}) collective-permute-start(bf16[288,384]{1,0:T(8,128)(2,1)S(1)} %polynomial.1), channel_id=1, source_target_pairs={{0,4},{1,5},{2,6},{3,7},{4,0},{5,1},{6,2},{7,3},{8,12},{9,13},{10,... | collective-permute-start | bytes 663560 | tf_op jit(solution)/shard_map/ppermute | solution.py:61
  169.9 10.9 %collective-permute-start.48 = (bf16[288,384]{1,0:T(8,128)(2,1)S(1)}, bf16[288,384]{1,0:T(8,128)(2,1)S(1)}, u32[]{:S(2)}, u32[]{:S(2)}) collective-permute-start(bf16[288,384]{1,0:T(8,128)(2,1)S(1)} %polynomial.1), channel_id=1, source_target_pairs={{0,2},{1,3},{2,0},{3,1},{4,6},{5,7},{6,4},{7,5},{8,10},{9,11},{10,... | collective-permute-start | bytes 663560 | tf_op jit(solution)/shard_map/ppermute | solution.py:61
  (47 other events, 384.8 us)
where the time goes:
time: 188 us; the launch traced here: 187 us
  Pallas kernels  71.4 us (38%)
  starting transfers between devices  57.2 us (30%)
  waiting for transfers between devices  49.3 us (26%)
  local copies, waits for them, and re-layouts  6.35 us (3%)
  other arithmetic  1.89 us (1%)
    pallas_call x18, Pallas kernels, local_call(): pl.pallas_call(run, grid_spec=pltpu.PrefetchScalarGridSpec(num_scalar_pre...  71.4 us
    ppermute x24, starting transfers between devices, shift(): lax.ppermute(value, 'shard', [(i, (i + distance) % size) for i in range(s...  31.1 us
    ppermute x28, waiting for transfers between devices, flip(): return lax.ppermute(value, 'rep', [(i, i ^ mask) for i in range(size)])  26.4 us
    ppermute x28, starting transfers between devices, flip(): return lax.ppermute(value, 'rep', [(i, i ^ mask) for i in range(size)])  26.1 us
    ppermute x24, waiting for transfers between devices, shift(): lax.ppermute(value, 'shard', [(i, (i + distance) % size) for i in range(s...  22.9 us
    unnamed x38, local copies, waits for them, and re-layouts  4.94 us
  transfers between devices with their start and end apart: 52, of which 26 were waited for; matrix products, arithmetic and copies ran while one was open for 1% of the time, Pallas kernels for 15%

commit v1 on v0

--- a/solution.py
+++ b/solution.py
@@ -26,6 +26,8 @@
     "perceptron": 40,
     "attention_backward": 32,
     "attend_backward": 36,
+    "modulation": 48,
+    "pack": 48,
     "momenta": 32,
     "gram": 24,
     "polynomial": 20,
@@ -400,16 +402,21 @@
     @pl.when(step == pl.num_programs(0) - 1)
     def _():
         shard, low = ids[0], ids[1]
-        for j in range(GROUP):
-            span = pl.ds(pl.multiple_of((low ^ j) * rows, rows), rows)
-            for s in range(shards):
-                d = lax.rem(s - shard + shards, shards)
-                lanes = slice(s * width, (s + 1) * width)
-                piece = jnp.concatenate([total_up[span, lanes], total_down[span, lanes]], axis=1)
-                if j & 1:
-                    send[j // 2, d] = piece.astype(LOW)
-                else:
-                    keep[j // 2, d] = piece
+
+        @pl.loop(0, GROUP // 2)
+        def _(t):
+            for bit in range(2):
+                span = rows_at(low ^ (2 * t + bit), rows)
+                for s in range(shards):
+                    d = lax.rem(s - shard + shards, shards)
+                    lanes = slice(s * width, (s + 1) * width)
+                    piece = jnp.concatenate(
+                        [total_up[span, lanes], total_down[span, lanes]], axis=1
+                    )
+                    if bit:
+                        send[t, d] = piece.astype(LOW)
+                    else:
+                        keep[t, d] = piece
 
 
 def attention_backward(
@@ -489,22 +496,26 @@
     def _():
         shard, low = ids[0], ids[1]
         wide, narrow = 3 * D // shards, D // shards
-        for j in range(GROUP):
-            span = rows_at(low ^ j, rows)
-            whole_attend, whole_project = total_attend[span, :], total_project[span, :]
-            for s in range(shards):
-                d = lax.rem(s - shard + shards, shards)
-                piece = jnp.concatenate(
-                    [
-                        whole_attend[:, s * wide : (s + 1) * wide],
-                        whole_project[:, s * narrow : (s + 1) * narrow],
-                    ],
-                    axis=1,
-                )
-                if j & 1:
-                    send[j // 2, d] = piece.astype(LOW)
-                else:
-                    keep[j // 2, d] = piece
+
+        @pl.loop(0, GROUP // 2)
+        def _(t):
+            for bit in range(2):
+                span = rows_at(low ^ (2 * t + bit), rows)
+                whole_attend, whole_project = total_attend[span, :], total_project[span, :]
+                for s in range(shards):
+                    d = lax.rem(s - shard + shards, shards)
+                    piece = jnp.concatenate(
+                        [
+                            whole_attend[:, s * wide : (s + 1) * wide],
+                            whole_project[:, s * narrow : (s + 1) * narrow],
+                        ],
+                        axis=1,
+                    )
+                    if bit:
+                        send[t, d] = piece.astype(LOW)
+                    else:
+                        keep[t, d] = piece
+
         latents = grad_mod.shape[0]
         columns = [grad_mod[:, b, :] for b in range(2)] + [grad_mod_late[:, b, :] for b in range(4)]
         whole = jnp.concatenate(columns, axis=1).astype(LOW).astype(FULL)
@@ -742,10 +753,13 @@
         half = both[:, :D]
         return POLY_LINEAR * half + dot(mixing_deep, right_deep(half)), both[:, D:]
 
-    gram_ref[...] = gram
-    product_ref[...] = jnp.where(diagonal, 1.0, 0.0)
-
-    @pl.loop(0, NS_ITERS - 1)
+    mixing = POLY_CUBIC * gram + POLY_QUINTIC * dot(left_deep(gram), right_deep(gram))
+    mixing_deep = left_deep(mixing)
+    half = POLY_LINEAR * gram + dot(mixing_deep, right_deep(gram))
+    gram_ref[...] = POLY_LINEAR * half + dot(mixing_deep, right_deep(half))
+    product_ref[...] = jnp.where(diagonal, POLY_LINEAR, 0.0) + mixing
+
+    @pl.loop(0, NS_ITERS - 2)
     def _(step):
         gram, product = advance(gram_ref[...], product_ref[...])
         gram_ref[...] = gram

time: 188 us -> 187 us (level)
  no operation moved by 1% of the time
where the time goes in v1:
time: 187 us
  Pallas kernels  71.3 us (38%)
  starting transfers between devices  57.1 us (31%)
  waiting for transfers between devices  49.4 us (26%)
  local copies, waits for them, and re-layouts  6.35 us (3%)
  other arithmetic  1.89 us (1%)
    pallas_call x18, Pallas kernels, local_call(): pl.pallas_call(run, grid_spec=pltpu.PrefetchScalarGridSpec(num_scalar_pre...  71.3 us
    ppermute x24, starting transfers between devices, shift(): lax.ppermute(value, 'shard', [(i, (i + distance) % size) for i in range(s...  31 us
    ppermute x28, waiting for transfers between devices, flip(): return lax.ppermute(value, 'rep', [(i, i ^ mask) for i in range(size)])  26.4 us
    ppermute x28, starting transfers between devices, flip(): return lax.ppermute(value, 'rep', [(i, i ^ mask) for i in range(size)])  26.1 us
    ppermute x24, waiting for transfers between devices, shift(): lax.ppermute(value, 'shard', [(i, (i + distance) % size) for i in range(s...  23 us
    unnamed x38, local copies, waits for them, and re-layouts  4.94 us
  transfers between devices with their start and end apart: 52, of which 26 were waited for; matrix products, arithmetic and copies ran while one was open for 1% of the time, Pallas kernels for 15%

profile of v1, /device:TPU:0, one launch (start us, length us, event | category | flops | bytes accessed | tf_op | source)
XLA Modules:
  0.0 187.1 jit_solution(1360964537827520580)
XLA Ops:
  4.7 5.1 %collective-permute-start.2 = (bf16[64,384]{1,0:T(8,128)(2,1)S(1)}, bf16[64,384]{1,0:T(8,128)(2,1)S(1)}, u32[]{:S(2)}, u32[]{:S(2)}) collective-permute-start(bf16[64,384]{1,0:T(8,128)(2,1)S(1)} %prepare.1.refs_1_.refs_8_.refs_5_), channel_id=1, source_target_pairs={{0,24},{8,0},{16,8},{24,16},{1,25},{9,1},{17,9},{25,17},{2,26},{10... | collective-permute-start | bytes 147464 | tf_op jit(solution)/shard_map/ppermute | solution.py:58
  11.9 2.9 %collective-permute-done.1.refs_3_.refs_10_.refs_7_ = bf16[64,384]{1,0:T(8,128)(2,1)S(1)} collective-permute-done((bf16[64,384]{1,0:T(8,128)(2,1)S(1)}, bf16[64,384]{1,0:T(8,128)(2,1)S(1)}, u32[]{:S(2)}, u32[]{:S(2)}) %collective-permute-start.1) | collective-permute-done | bytes 49184 | tf_op jit(solution)/shard_map/ppermute | solution.py:58
  22.9 2.4 %collective-permute-start.5 = (bf16[4,48,384]{2,1,0:T(8,128)(2,1)S(1)}, bf16[4,48,384]{2,1,0:T(8,128)(2,1)S(1)}, u32[]{:S(2)}, u32[]{:S(2)}) collective-permute-start(bf16[4,48,384]{2,1,0:T(8,128)(2,1)S(1)} %get-tuple-element.85.refs_3_.refs_1_), channel_id=1, source_target_pairs={{0,6},{1,7},{2,4},{3,5},{4,2},{5,3},{6,0},{7,1},{8,14},{9,15},{10,... | collective-permute-start | bytes 442376 | tf_op jit(solution)/shard_map/ppermute | solution.py:63
  28.0 2.5 %collective-permute-done.5.refs_4_ = bf16[4,48,384]{2,1,0:T(8,128)(2,1)S(1)} collective-permute-done((bf16[4,48,384]{2,1,0:T(8,128)(2,1)S(1)}, bf16[4,48,384]{2,1,0:T(8,128)(2,1)S(1)}, u32[]{:S(2)}, u32[]{:S(2)}) %collective-permute-start.5) | collective-permute-done | bytes 147488 | tf_op jit(solution)/shard_map/ppermute | solution.py:63
  31.9 2.1 %collective-permute-start.10 = (f32[4,576]{1,0:T(4,128)S(1)}, f32[4,576]{1,0:T(4,128)S(1)}, u32[]{:S(2)}, u32[]{:S(2)}) collective-permute-start(f32[4,576]{1,0:T(4,128)S(1)} %get-tuple-element.87), channel_id=1, source_target_pairs={{0,24},{8,0},{16,8},{24,16},{1,25},{9,1},{17,9},{25,17},{2,26},{10... | collective-permute-start | bytes 27656 | tf_op jit(solution)/shard_map/ppermute | solution.py:58
  40.3 13.0 %attention_forward.1 = (bf16[4,256,1152]{2,1,0:T(8,128)(2,1)S(1)}, bf16[4,6,256,256]{3,2,1,0:T(8,128)(2,1)S(1)}, bf16[4,256,384]{2,1,0:T(8,128)(2,1)S(1)}, f32[4...) custom-call(s32[2]{0:T(128)S(1)} %pad_add_fusion.refs_0_, ...), custom_call_target="tpu_custom_call" | custom-call | flops 4026531840 | bytes 11288064 | tf_op jit(solution)/shard_map/attention_forward/pallas_call | solution.py:158
  54.0 2.8 %collective-permute-done.16.refs_6_ = bf16[4,4,48,768]{3,2,1,0:T(8,128)(2,1)S(1)} collective-permute-done((bf16[4,4,48,768]{3,2,1,0:T(8,128)(2,1)S(1)}, bf16[4,4,48,768]{3,2,1,0:T(8,128)(2,1)S(1)}, u32[]{:S(2)}, u32[]{:S(2)}) %collective-permute-start.16) | collective-permute-done | bytes 1179680 | tf_op jit(solution)/shard_map/ppermute | solution.py:63
  56.8 13.9 %perceptron.1 = (bf16[4,256,384]{2,1,0:T(8,128)(2,1)}, f32[4,256,384]{2,1,0:T(8,128)S(1)}, f32[4,4,384]{2,1,0:T(4,128)S(1)}, f32[4,4,48,768]{3,2,1,0:T(8,128)S(1...) custom-call(s32[2]{0:T(128)S(1)} %pad_add_fusion.refs_0_, ...), custom_call_target="tpu_custom_call" | custom-call | flops 14495514624 | bytes 11480064 | tf_op jit(solution)/shard_map/perceptron/pallas_call | solution.py:158
  70.9 2.7 %collective-permute-done.17.refs_2_ = bf16[4,4,48,768]{3,2,1,0:T(8,128)(2,1)S(1)} collective-permute-done((bf16[4,4,48,768]{3,2,1,0:T(8,128)(2,1)S(1)}, bf16[4,4,48,768]{3,2,1,0:T(8,128)(2,1)S(1)}, u32[]{:S(2)}, u32[]{:S(2)}) %collective-permute-start.17) | collective-permute-done | bytes 1179680 | tf_op jit(solution)/shard_map/ppermute | solution.py:63
  78.0 10.6 %attention_backward.1 = (bf16[4,256,1152]{2,1,0:T(8,128)(2,1)S(1)}, f32[384,384]{1,0:T(8,128)S(1)}) custom-call(s32[2]{0:T(128)S(1)} %pad_add_fusion.refs_0_, f32[4,6,384]{2,1,0:T(8,128)S(1)} %get-tuple-element.91.refs_3_.refs_1_.refs_2_, bf16[4,256,384]{2,1,0:T(8,128)(2,1)S(1)} %get-tuple-element.96.refs_2_, f32[4,256,384]{2,1,0:T(8,128)S(1)} %get-tuple-element.95.refs_3_, ...), custom_call_target="tpu_custom_call" | custom-call | flops 2617245696 | bytes 11145216 | tf_op jit(solution)/shard_map/attention_backward/pallas_call | solution.py:158
  90.9 6.6 %attend_backward.1 = (f32[4,256,384]{2,1,0:T(8,128)}, f32[4,4,48,384]{3,2,1,0:T(8,128)S(1)}, bf16[4,4,48,384]{3,2,1,0:T(8,128)(2,1)S(1)}, bf16[4,16,384]{2,1,0:T(8,128)(2,1)S(1)}) custom-call(s32[2]{0:T(128)S(1)} %pad_add_fusion.refs_0_, bf16[4,256,384]{2,1,0:T(8,128)(2,1)S(1)} %copy-done.18, f32[4,6,384]{2,1,0:T(8,128)S(1)} %get-tuple-element.91.refs_3_.refs_1_.refs_2_, ...), custom_call_target="tpu_custom_call" | custom-call | flops 3623878656 | bytes 9653760 | tf_op jit(solution)/shard_map/attend_backward/pallas_call | solution.py:158
  97.5 1.9 %collective-permute-start.27 = (bf16[48,768]{1,0:T(8,128)(2,1)S(1)}, bf16[48,768]{1,0:T(8,128)(2,1)S(1)}, u32[]{:S(2)}, u32[]{:S(2)}) collective-permute-start(bf16[48,768]{1,0:T(8,128)(2,1)S(1)} %get-tuple-element.157), channel_id=1, source_target_pairs={{0,24},{8,0},{16,8},{24,16},{1,25},{9,1},{17,9},{25,17},{2,26},{10... | collective-permute-start | bytes 221192 | tf_op jit(solution)/shard_map/ppermute | solution.py:58
  104.6 3.0 %collective-permute-done.26.refs_3_ = bf16[48,768]{1,0:T(8,128)(2,1)S(1)} collective-permute-done((bf16[48,768]{1,0:T(8,128)(2,1)S(1)}, bf16[48,768]{1,0:T(8,128)(2,1)S(1)}, u32[]{:S(2)}, u32[]{:S(2)}) %collective-permute-start.26) | collective-permute-done | bytes 73760 | tf_op jit(solution)/shard_map/ppermute | solution.py:58
  112.4 2.0 %collective-permute-start.28 = (bf16[64,384]{1,0:T(8,128)(2,1)S(1)}, bf16[64,384]{1,0:T(8,128)(2,1)S(1)}, u32[]{:S(2)}, u32[]{:S(2)}) collective-permute-start(bf16[64,384]{1,0:T(8,128)(2,1)S(1)} %get-tuple-element.121), channel_id=1, source_target_pairs={{0,8},{8,16},{16,24},{24,0},{1,9},{9,17},{17,25},{25,1},{2,10},{10... | collective-permute-start | bytes 147464 | tf_op jit(solution)/shard_map/ppermute | solution.py:58
  121.2 2.5 %collective-permute-start.39 = (bf16[112,384]{1,0:T(8,128)(2,1)S(1)}, bf16[112,384]{1,0:T(8,128)(2,1)S(1)}, u32[]{:S(2)}, u32[]{:S(2)}) collective-permute-start(bf16[112,384]{1,0:T(8,128)(2,1)S(1)} %get-tuple-element.129), channel_id=1, source_target_pairs={{0,6},{1,7},{2,4},{3,5},{4,2},{5,3},{6,0},{7,1},{8,14},{9,15},{10,... | collective-permute-start | bytes 258056 | tf_op jit(solution)/shard_map/ppermute | solution.py:63
  130.8 2.0 %gram.1 = (f32[4,192,128]{2,1,0:T(8,128)S(1)}, f32[288,384]{1,0:T(8,128)S(1)}) custom-call(s32[2]{0:T(128)S(1)} %pad_add_fusion.refs_0_, bf16[4,112,384]{2,1,0:T(8,128)(2,1)S(1)} %pad_maximum_fusion.1.refs_1_, bf16[4,112,384]{2,1,0:T(8,128)(2,1)S(1)} %collective-permute-done.40.refs_2_, bf16[4,48,768]{2,1,0:T(8,128)(2,1)S(1)} %pad_maximum_fusion.3.refs_10_.refs_3_, ...), custom_call_target="tpu_custom_call" | custom-call | flops 339738624 | bytes 4767744 | tf_op jit(solution)/shard_map/gram/pallas_call | solution.py:158
  133.4 3.3 %collective-permute-start.44 = (f32[192,128]{1,0:T(8,128)S(1)}, f32[192,128]{1,0:T(8,128)S(1)}, u32[]{:S(2)}, u32[]{:S(2)}) collective-permute-start(f32[192,128]{1,0:T(8,128)S(1)} %get-tuple-element.155), channel_id=1, source_target_pairs={{0,24},{8,0},{16,8},{24,16},{1,25},{9,1},{17,9},{25,17},{2,26},{10... | collective-permute-start | bytes 294920 | tf_op jit(solution)/shard_map/ppermute | solution.py:58
  141.6 4.0 %collective-permute-done.43 = f32[192,128]{1,0:T(8,128)S(1)} collective-permute-done((f32[192,128]{1,0:T(8,128)S(1)}, f32[192,128]{1,0:T(8,128)S(1)}, u32[]{:S(2)}, u32[]{:S(2)}) %collective-permute-start.43) | collective-permute-done | bytes 98336 | tf_op jit(solution)/shard_map/ppermute | solution.py:58
  148.2 3.4 %momenta.1 = (f32[288,384]{1,0:T(8,128)}, f32[96,384]{1,0:T(8,128)}, f32[384,384]{1,0:T(8,128)}, f32[384,384]{1,0:T(8,128)}, f32[576,384]{1,0:T(8,128)}, /*index...) custom-call(s32[2]{0:T(128)S(1)} %pad_add_fusion.refs_0_, ...), custom_call_target="tpu_custom_call" | custom-call | flops 56623104 | bytes 9252864 | tf_op jit(solution)/shard_map/momenta/pallas_call | solution.py:158
  151.6 4.8 %collective-permute-done.46.refs_3_ = f32[192,128]{1,0:T(8,128)S(1)} collective-permute-done((f32[192,128]{1,0:T(8,128)S(1)}, f32[192,128]{1,0:T(8,128)S(1)}, u32[]{:S(2)}, u32[]{:S(2)}) %collective-permute-start.46) | collective-permute-done | bytes 98336 | tf_op jit(solution)/shard_map/ppermute | solution.py:58
  156.4 11.2 %polynomial.1 = bf16[288,384]{1,0:T(8,128)(2,1)S(1)} custom-call(s32[2]{0:T(128)S(1)} %pad_add_fusion.refs_0_, f32[192,128]{1,0:T(8,128)S(1)} %fusion.1.refs_1_, f32[192,128]{1,0:T(8,128)S(1)} %collective-permute-done.45.refs_2_, f32[192,128]{1,0:T(8,128)S(1)} %collective-permute-done.46.refs_3_, f32[192,128]{1,0:T(8,128)S(1)} %collective-permute-done.47.refs_4_, ...), custom_call_target="tpu_custom_call" | custom-call | flops 6115295232 | bytes 1056768 | tf_op jit(solution)/shard_map/polynomial/pallas_call | solution.py:158
  171.3 5.8 %collective-permute-done.50 = bf16[288,384]{1,0:T(8,128)(2,1)S(1)} collective-permute-done((bf16[288,384]{1,0:T(8,128)(2,1)S(1)}, bf16[288,384]{1,0:T(8,128)(2,1)S(1)}, u32[]{:S(2)}, u32[]{:S(2)}) %collective-permute-start.50) | collective-permute-done | bytes 221216 | tf_op jit(solution)/shard_map/ppermute | solution.py:63
  177.0 3.7 %collective-permute-done.49 = bf16[288,384]{1,0:T(8,128)(2,1)S(1)} collective-permute-done((bf16[288,384]{1,0:T(8,128)(2,1)S(1)}, bf16[288,384]{1,0:T(8,128)(2,1)S(1)}, u32[]{:S(2)}, u32[]{:S(2)}) %collective-permute-start.49) | collective-permute-done | bytes 221216 | tf_op jit(solution)/shard_map/ppermute | solution.py:63
  183.5 3.6 %update.1 = (f32[288,384]{1,0:T(8,128)}, f32[96,384]{1,0:T(8,128)}, f32[384,384]{1,0:T(8,128)}, f32[384,384]{1,0:T(8,128)}, f32[576,384]{1,0:T(8,128)}) custom-call(s32[2]{0:T(128)S(1)} %pad_add_fusion.refs_0_, bf16[4,288,384]{2,1,0:T(8,128)(2,1)S(1)} %pad_maximum_fusion.refs_1_, bf16[4,288,384]{2,1,0:T(8,128)(2,1)} %collective-permute-done.51.refs_2_, ...), custom_call_target="tpu_custom_call" | custom-call | flops 1327104 | bytes 7077888 | tf_op jit(solution)/shard_map/update/pallas_call | solution.py:158
  (150 shorter events, 70.1 us)
Async XLA Ops:
  22.9 7.7 %collective-permute-start.5 = (bf16[4,48,384]{2,1,0:T(8,128)(2,1)S(1)}, bf16[4,48,384]{2,1,0:T(8,128)(2,1)S(1)}, u32[]{:S(2)}, u32[]{:S(2)}) collective-permute-start(bf16[4,48,384]{2,1,0:T(8,128)(2,1)S(1)} %get-tuple-element.85.refs_3_.refs_1_), channel_id=1, source_target_pairs={{0,6},{1,7},{2,4},{3,5},{4,2},{5,3},{6,0},{7,1},{8,14},{9,15},{10,... | collective-permute-start | bytes 442376 | tf_op jit(solution)/shard_map/ppermute | solution.py:63
  31.9 8.4 %collective-permute-start.9 = (bf16[4,4,48,384]{3,2,1,0:T(8,128)(2,1)S(1)}, bf16[4,4,48,384]{3,2,1,0:T(8,128)(2,1)S(1)}, u32[]{:S(2)}, u32[]{:S(2)}) collective-permute-start(bf16[4,4,48,384]{3,2,1,0:T(8,128)(2,1)S(1)} %stack_late.1.refs_2_), channel_id=1, source_target_pairs={{0,1},{1,0},{2,3},{3,2},{4,5},{5,4},{6,7},{7,6},{8,9},{9,8},{10,11... | collective-permute-start | bytes 1769480 | tf_op jit(solution)/shard_map/ppermute | solution.py:63
  35.7 17.6 %collective-permute-start.15 = (bf16[4,48,768]{2,1,0:T(8,128)(2,1)S(1)}, bf16[4,48,768]{2,1,0:T(8,128)(2,1)S(1)}, u32[]{:S(2)}, u32[]{:S(2)}) collective-permute-start(bf16[4,48,768]{2,1,0:T(8,128)(2,1)S(1)} %pad_maximum_fusion.2.refs_5_.refs_12_.refs_1_), channel_id=1, source_target_pairs={{0,6},{1,7},{2,4},{3,5},{4,2},{5,3},{6,0},{7,1},{8,14},{9,15},{10,... | collective-permute-start | bytes 884744 | tf_op jit(solution)/shard_map/ppermute | solution.py:63
  37.1 16.2 %collective-permute-start.14 = (bf16[4,48,768]{2,1,0:T(8,128)(2,1)S(1)}, bf16[4,48,768]{2,1,0:T(8,128)(2,1)S(1)}, u32[]{:S(2)}, u32[]{:S(2)}) collective-permute-start(bf16[4,48,768]{2,1,0:T(8,128)(2,1)S(1)} %pad_maximum_fusion.2.refs_5_.refs_12_.refs_1_), channel_id=1, source_target_pairs={{0,4},{1,5},{2,6},{3,7},{4,0},{5,1},{6,2},{7,3},{8,12},{9,13},{10,... | collective-permute-start | bytes 884744 | tf_op jit(solution)/shard_map/ppermute | solution.py:63
  38.6 14.6 %collective-permute-start.13 = (bf16[4,48,768]{2,1,0:T(8,128)(2,1)S(1)}, bf16[4,48,768]{2,1,0:T(8,128)(2,1)S(1)}, u32[]{:S(2)}, u32[]{:S(2)}) collective-permute-start(bf16[4,48,768]{2,1,0:T(8,128)(2,1)S(1)} %pad_maximum_fusion.2.refs_5_.refs_12_.refs_1_), channel_id=1, source_target_pairs={{0,2},{1,3},{2,0},{3,1},{4,6},{5,7},{6,4},{7,5},{8,10},{9,11},{10,... | collective-permute-start | bytes 884744 | tf_op jit(solution)/shard_map/ppermute | solution.py:63
  74.4 14.1 %collective-permute-start.18 = (bf16[4,48,768]{2,1,0:T(8,128)(2,1)S(1)}, bf16[4,48,768]{2,1,0:T(8,128)(2,1)S(1)}, u32[]{:S(2)}, u32[]{:S(2)}) collective-permute-start(bf16[4,48,768]{2,1,0:T(8,128)(2,1)S(1)} %get-tuple-element.102.refs_7_), channel_id=1, source_target_pairs={{0,2},{1,3},{2,0},{3,1},{4,6},{5,7},{6,4},{7,5},{8,10},{9,11},{10,... | collective-permute-start | bytes 884744 | tf_op jit(solution)/shard_map/ppermute | solution.py:63
  75.5 13.7 %collective-permute-start.19 = (bf16[4,48,768]{2,1,0:T(8,128)(2,1)S(1)}, bf16[4,48,768]{2,1,0:T(8,128)(2,1)S(1)}, u32[]{:S(2)}, u32[]{:S(2)}) collective-permute-start(bf16[4,48,768]{2,1,0:T(8,128)(2,1)S(1)} %get-tuple-element.103.refs_8_), channel_id=1, source_target_pairs={{0,4},{1,5},{2,6},{3,7},{4,0},{5,1},{6,2},{7,3},{8,12},{9,13},{10,... | collective-permute-start | bytes 884744 | tf_op jit(solution)/shard_map/ppermute | solution.py:63
  76.5 14.2 %collective-permute-start.20 = (bf16[4,48,768]{2,1,0:T(8,128)(2,1)S(1)}, bf16[4,48,768]{2,1,0:T(8,128)(2,1)S(1)}, u32[]{:S(2)}, u32[]{:S(2)}) collective-permute-start(bf16[4,48,768]{2,1,0:T(8,128)(2,1)S(1)} %get-tuple-element.104.refs_9_), channel_id=1, source_target_pairs={{0,6},{1,7},{2,4},{3,5},{4,2},{5,3},{6,0},{7,1},{8,14},{9,15},{10,... | collective-permute-start | bytes 884744 | tf_op jit(solution)/shard_map/ppermute | solution.py:63
  99.4 8.2 %collective-permute-start.26 = (bf16[48,768]{1,0:T(8,128)(2,1)S(1)}, bf16[48,768]{1,0:T(8,128)(2,1)S(1)}, u32[]{:S(2)}, u32[]{:S(2)}) collective-permute-start(bf16[48,768]{1,0:T(8,128)(2,1)S(1)} %get-tuple-element.158), channel_id=1, source_target_pairs={{0,16},{8,24},{16,0},{24,8},{1,17},{9,25},{17,1},{25,9},{2,18},{10... | collective-permute-start | bytes 221192 | tf_op jit(solution)/shard_map/ppermute | solution.py:58
  101.0 9.4 %collective-permute-start.22 = (bf16[4,48,384]{2,1,0:T(8,128)(2,1)S(1)}, bf16[4,48,384]{2,1,0:T(8,128)(2,1)S(1)}, u32[]{:S(2)}, u32[]{:S(2)}) collective-permute-start(bf16[4,48,384]{2,1,0:T(8,128)(2,1)S(1)} %get-tuple-element.116.refs_5_), channel_id=1, source_target_pairs={{0,2},{1,3},{2,0},{3,1},{4,6},{5,7},{6,4},{7,5},{8,10},{9,11},{10,... | collective-permute-start | bytes 442376 | tf_op jit(solution)/shard_map/ppermute | solution.py:63
  101.7 10.0 %collective-permute-start.23 = (bf16[4,48,384]{2,1,0:T(8,128)(2,1)S(1)}, bf16[4,48,384]{2,1,0:T(8,128)(2,1)S(1)}, u32[]{:S(2)}, u32[]{:S(2)}) collective-permute-start(bf16[4,48,384]{2,1,0:T(8,128)(2,1)S(1)} %get-tuple-element.117.refs_6_), channel_id=1, source_target_pairs={{0,4},{1,5},{2,6},{3,7},{4,0},{5,1},{6,2},{7,3},{8,12},{9,13},{10,... | collective-permute-start | bytes 442376 | tf_op jit(solution)/shard_map/ppermute | solution.py:63
  103.1 8.6 %collective-permute-start.24 = (bf16[4,48,384]{2,1,0:T(8,128)(2,1)S(1)}, bf16[4,48,384]{2,1,0:T(8,128)(2,1)S(1)}, u32[]{:S(2)}, u32[]{:S(2)}) collective-permute-start(bf16[4,48,384]{2,1,0:T(8,128)(2,1)S(1)} %get-tuple-element.118.refs_7_), channel_id=1, source_target_pairs={{0,6},{1,7},{2,4},{3,5},{4,2},{5,3},{6,0},{7,1},{8,14},{9,15},{10,... | collective-permute-start | bytes 442376 | tf_op jit(solution)/shard_map/ppermute | solution.py:63
  108.2 8.0 %collective-permute-start.33 = (bf16[48,768]{1,0:T(8,128)(2,1)S(1)}, bf16[48,768]{1,0:T(8,128)(2,1)S(1)}, u32[]{:S(2)}, u32[]{:S(2)}) collective-permute-start(bf16[48,768]{1,0:T(8,128)(2,1)S(1)} %early_total.1.refs_6_), channel_id=1, source_target_pairs={{0,6},{1,7},{2,4},{3,5},{4,2},{5,3},{6,0},{7,1},{8,14},{9,15},{10,... | collective-permute-start | bytes 221192 | tf_op jit(solution)/shard_map/ppermute | solution.py:63
  132.8 7.5 %collective-permute-start.42 = (f32[192,128]{1,0:T(8,128)S(1)}, f32[192,128]{1,0:T(8,128)S(1)}, u32[]{:S(2)}, u32[]{:S(2)}) collective-permute-start(f32[192,128]{1,0:T(8,128)S(1)} %get-tuple-element.154), channel_id=1, source_target_pairs={{0,8},{8,16},{16,24},{24,0},{1,9},{9,17},{17,25},{25,1},{2,10},{10... | collective-permute-start | bytes 294920 | tf_op jit(solution)/shard_map/ppermute | solution.py:58
  133.4 8.2 %collective-permute-start.44 = (f32[192,128]{1,0:T(8,128)S(1)}, f32[192,128]{1,0:T(8,128)S(1)}, u32[]{:S(2)}, u32[]{:S(2)}) collective-permute-start(f32[192,128]{1,0:T(8,128)S(1)} %get-tuple-element.155), channel_id=1, source_target_pairs={{0,24},{8,0},{16,8},{24,16},{1,25},{9,1},{17,9},{25,17},{2,26},{10... | collective-permute-start | bytes 294920 | tf_op jit(solution)/shard_map/ppermute | solution.py:58
  136.7 9.0 %collective-permute-start.43 = (f32[192,128]{1,0:T(8,128)S(1)}, f32[192,128]{1,0:T(8,128)S(1)}, u32[]{:S(2)}, u32[]{:S(2)}) collective-permute-start(f32[192,128]{1,0:T(8,128)S(1)} %get-tuple-element.156), channel_id=1, source_target_pairs={{0,16},{8,24},{16,0},{24,8},{1,17},{9,25},{17,1},{25,9},{2,18},{10... | collective-permute-start | bytes 294920 | tf_op jit(solution)/shard_map/ppermute | solution.py:58
  136.7 10.9 %collective-permute-start.34 = (f32[4,384]{1,0:T(4,128)S(1)}, f32[4,384]{1,0:T(4,128)S(1)}, u32[]{:S(2)}, u32[]{:S(2)}) collective-permute-start(f32[4,384]{1,0:T(4,128)S(1)} %get-tuple-element.126), channel_id=1, source_target_pairs={{0,24},{8,0},{16,8},{24,16},{1,25},{9,1},{17,9},{25,17},{2,26},{10... | collective-permute-start | bytes 18440 | tf_op jit(solution)/shard_map/ppermute | solution.py:58
  137.8 10.4 %collective-permute-start.35 = (f32[4,384]{1,0:T(4,128)S(1)}, f32[4,384]{1,0:T(4,128)S(1)}, u32[]{:S(2)}, u32[]{:S(2)}) collective-permute-start(f32[4,384]{1,0:T(4,128)S(1)} %get-tuple-element.127), channel_id=1, source_target_pairs={{0,16},{8,24},{16,0},{24,8},{1,17},{9,25},{17,1},{25,9},{2,18},{10... | collective-permute-start | bytes 18440 | tf_op jit(solution)/shard_map/ppermute | solution.py:58
  140.3 7.9 %collective-permute-start.36 = (f32[4,384]{1,0:T(4,128)S(1)}, f32[4,384]{1,0:T(4,128)S(1)}, u32[]{:S(2)}, u32[]{:S(2)}) collective-permute-start(f32[4,384]{1,0:T(4,128)S(1)} %get-tuple-element.128), channel_id=1, source_target_pairs={{0,8},{8,16},{16,24},{24,0},{1,9},{9,17},{17,25},{25,1},{2,10},{10... | collective-permute-start | bytes 18440 | tf_op jit(solution)/shard_map/ppermute | solution.py:58
  147.5 8.9 %collective-permute-start.46 = (f32[192,128]{1,0:T(8,128)S(1)}, f32[192,128]{1,0:T(8,128)S(1)}, u32[]{:S(2)}, u32[]{:S(2)}) collective-permute-start(f32[192,128]{1,0:T(8,128)S(1)} %fusion.1.refs_1_), channel_id=1, source_target_pairs={{0,16},{8,24},{16,0},{24,8},{1,17},{9,25},{17,1},{25,9},{2,18},{10... | collective-permute-start | bytes 294920 | tf_op jit(solution)/shard_map/ppermute | solution.py:58
  147.5 8.9 %collective-permute-start.45 = (f32[192,128]{1,0:T(8,128)S(1)}, f32[192,128]{1,0:T(8,128)S(1)}, u32[]{:S(2)}, u32[]{:S(2)}) collective-permute-start(f32[192,128]{1,0:T(8,128)S(1)} %fusion.1.refs_1_), channel_id=1, source_target_pairs={{0,8},{8,16},{16,24},{24,0},{1,9},{9,17},{17,25},{25,1},{2,10},{10... | collective-permute-start | bytes 294920 | tf_op jit(solution)/shard_map/ppermute | solution.py:58
  167.7 9.3 %collective-permute-start.50 = (bf16[288,384]{1,0:T(8,128)(2,1)S(1)}, bf16[288,384]{1,0:T(8,128)(2,1)S(1)}, u32[]{:S(2)}, u32[]{:S(2)}) collective-permute-start(bf16[288,384]{1,0:T(8,128)(2,1)S(1)} %polynomial.1), channel_id=1, source_target_pairs={{0,6},{1,7},{2,4},{3,5},{4,2},{5,3},{6,0},{7,1},{8,14},{9,15},{10,... | collective-permute-start | bytes 663560 | tf_op jit(solution)/shard_map/ppermute | solution.py:63
  169.5 11.2 %collective-permute-start.49 = (bf16[288,384]{1,0:T(8,128)(2,1)S(1)}, bf16[288,384]{1,0:T(8,128)(2,1)S(1)}, u32[]{:S(2)}, u32[]{:S(2)}) collective-permute-start(bf16[288,384]{1,0:T(8,128)(2,1)S(1)} %polynomial.1), channel_id=1, source_target_pairs={{0,4},{1,5},{2,6},{3,7},{4,0},{5,1},{6,2},{7,3},{8,12},{9,13},{10,... | collective-permute-start | bytes 663560 | tf_op jit(solution)/shard_map/ppermute | solution.py:63
  169.7 11.0 %collective-permute-start.48 = (bf16[288,384]{1,0:T(8,128)(2,1)S(1)}, bf16[288,384]{1,0:T(8,128)(2,1)S(1)}, u32[]{:S(2)}, u32[]{:S(2)}) collective-permute-start(bf16[288,384]{1,0:T(8,128)(2,1)S(1)} %polynomial.1), channel_id=1, source_target_pairs={{0,2},{1,3},{2,0},{3,1},{4,6},{5,7},{6,4},{7,5},{8,10},{9,11},{10,... | collective-permute-start | bytes 663560 | tf_op jit(solution)/shard_map/ppermute | solution.py:63
  (47 other events, 384.2 us)

commit v2 on v1

--- a/solution.py
+++ b/solution.py
@@ -852,6 +852,18 @@
     )
     notes = exchange([note] * shards)
 
+    (early_weights,) = local_call(
+        pack,
+        ids,
+        [(w, (rows, lambda place: place)) for w in (expand_weight, contract_weight)],
+        [((rows, 2 * FF // shards), LOW, False)],
+        [],
+        1,
+        D * D,
+        "pack",
+    )
+    early_weights = exchange([early_weights] * shards)
+
     *shares, modulate_low, late_weights = local_call(
         modulation_kernel,
         ids,
@@ -862,22 +874,10 @@
         1,
         2 * shards * NOTE * D * mod_share,
         "modulation",
+        after=tuple(early_weights[1:]),
     )
     answers = [shares[0]] + [shift(shares[d], shards - d) for d in range(1, shards)]
     late_weights_chips = gather_chips(late_weights)
-    (early_weights,) = local_call(
-        pack,
-        ids,
-        [(w, (rows, lambda place: place)) for w in (expand_weight, contract_weight)],
-        [((rows, 2 * FF // shards), LOW, False)],
-        [],
-        1,
-        D * D,
-        "pack",
-        after=(late_weights,),
-    )
-    early_weights = jnp.stack(exchange([early_weights] * shards))
-    early_weights_chips = gather_chips(early_weights)
     (late_stacked,) = local_call(
         stack,
         ids,
@@ -887,9 +887,21 @@
         1,
         D * D,
         "stack_late",
-        after=(early_weights,),
+        after=tuple(answers[1:]),
     )
     late_flipped = flip(late_stacked, 1)
+    (early_weights,) = local_call(
+        stack,
+        ids,
+        [(v, False) for v in early_weights],
+        [((shards, rows, 2 * FF // shards), LOW, False)],
+        [],
+        1,
+        D * D,
+        "stack_early",
+        after=(late_stacked,),
+    )
+    early_weights_chips = gather_chips(early_weights)
 
     tokens_shape = (latents, LEN, D)
     qkv, probs, attended, branch, wq, wo, mod, bias_up, bias_down = local_call(

time: 187 us -> 190 us (1.016)
  waiting for transfers between devices: 49.4 us -> 53.1 us
    ppermute x24, waiting for transfers between devices: 23 us -> 29.6 us  [shift(): lax.ppermute(value, 'shard', [(i, (i + distance) % size) for i in range(s...]
    ppermute x28, waiting for transfers between devices: 26.4 us -> 23.5 us  [flip(): return lax.ppermute(value, 'rep', [(i, i ^ mask) for i in range(size)])]
    pallas_call x18 -> x19, Pallas kernels: 71.3 us -> 71.8 us  [local_call(): pl.pallas_call(run, grid_spec=pltpu.PrefetchScalarGridSpec(num_scalar_pre...]
    unnamed x38 -> x42, local copies, waits for them, and re-layouts: 4.94 us -> 4.84 us
  transfers between devices with their start and end apart: 52 -> 52, of which waited for: 26 -> 23; matrix products, arithmetic and copies ran while one was open for 1% -> 1% of each run, Pallas kernels for 15% -> 16%
where the time goes in v2:
time: 190 us
  Pallas kernels  71.8 us (38%)
  starting transfers between devices  55.8 us (29%)
  waiting for transfers between devices  53.1 us (28%)
  local copies, waits for them, and re-layouts  6.26 us (3%)
    pallas_call x19, Pallas kernels, local_call(): pl.pallas_call(run, grid_spec=pltpu.PrefetchScalarGridSpec(num_scalar_pre...  71.8 us
    ppermute x24, starting transfers between devices, shift(): lax.ppermute(value, 'shard', [(i, (i + distance) % size) for i in range(s...  30 us
    ppermute x24, waiting for transfers between devices, shift(): lax.ppermute(value, 'shard', [(i, (i + distance) % size) for i in range(s...  29.6 us
    ppermute x28, starting transfers between devices, flip(): return lax.ppermute(value, 'rep', [(i, i ^ mask) for i in range(size)])  25.7 us
    ppermute x28, waiting for transfers between devices, flip(): return lax.ppermute(value, 'rep', [(i, i ^ mask) for i in range(size)])  23.5 us
    unnamed x42, local copies, waits for them, and re-layouts  4.84 us
  transfers between devices with their start and end apart: 52, of which 23 were waited for; matrix products, arithmetic and copies ran while one was open for 1% of the time, Pallas kernels for 16%

profile of v2, /device:TPU:0, one launch (start us, length us, event | category | flops | bytes accessed | tf_op | source)
XLA Modules:
  0.0 189.9 jit_solution(9336593356800880338)
XLA Ops:
  4.7 5.1 %collective-permute-start.2 = (bf16[64,384]{1,0:T(8,128)(2,1)S(1)}, bf16[64,384]{1,0:T(8,128)(2,1)S(1)}, u32[]{:S(2)}, u32[]{:S(2)}) collective-permute-start(bf16[64,384]{1,0:T(8,128)(2,1)S(1)} %prepare.1.refs_1_.refs_8_.refs_5_), channel_id=1, source_target_pairs={{0,24},{8,0},{16,8},{24,16},{1,25},{9,1},{17,9},{25,17},{2,26},{10... | collective-permute-start | bytes 147464 | tf_op jit(solution)/shard_map/ppermute | solution.py:58
  14.6 2.9 %collective-permute-start.1 = (bf16[64,384]{1,0:T(8,128)(2,1)S(1)}, bf16[64,384]{1,0:T(8,128)(2,1)S(1)}, u32[]{:S(2)}, u32[]{:S(2)}) collective-permute-start(bf16[64,384]{1,0:T(8,128)(2,1)S(1)} %prepare.1.refs_1_.refs_8_.refs_5_), channel_id=1, source_target_pairs={{0,16},{8,24},{16,0},{24,8},{1,17},{9,25},{17,1},{25,9},{2,18},{10... | collective-permute-start | bytes 147464 | tf_op jit(solution)/shard_map/ppermute | solution.py:58
  17.5 6.4 %collective-permute-done.1.refs_3_.refs_10_.refs_7_ = bf16[64,384]{1,0:T(8,128)(2,1)S(1)} collective-permute-done((bf16[64,384]{1,0:T(8,128)(2,1)S(1)}, bf16[64,384]{1,0:T(8,128)(2,1)S(1)}, u32[]{:S(2)}, u32[]{:S(2)}) %collective-permute-start.1) | collective-permute-done | bytes 49184 | tf_op jit(solution)/shard_map/ppermute | solution.py:58
  25.1 2.5 %collective-permute-start.8 = (bf16[4,48,384]{2,1,0:T(8,128)(2,1)S(1)}, bf16[4,48,384]{2,1,0:T(8,128)(2,1)S(1)}, u32[]{:S(2)}, u32[]{:S(2)}) collective-permute-start(bf16[4,48,384]{2,1,0:T(8,128)(2,1)S(1)} %get-tuple-element.85.refs_1_), channel_id=1, source_target_pairs={{0,6},{1,7},{2,4},{3,5},{4,2},{5,3},{6,0},{7,1},{8,14},{9,15},{10,... | collective-permute-start | bytes 442376 | tf_op jit(solution)/shard_map/ppermute | solution.py:63
  34.8 2.9 %collective-permute-done.11.refs_7_ = f32[4,576]{1,0:T(4,128)S(1)} collective-permute-done((f32[4,576]{1,0:T(4,128)S(1)}, f32[4,576]{1,0:T(4,128)S(1)}, u32[]{:S(2)}, u32[]{:S(2)}) %collective-permute-start.11) | collective-permute-done | bytes 9248 | tf_op jit(solution)/shard_map/ppermute | solution.py:58
  39.0 2.5 %collective-permute-start.15 = (bf16[4,48,768]{2,1,0:T(8,128)(2,1)S(1)}, bf16[4,48,768]{2,1,0:T(8,128)(2,1)S(1)}, u32[]{:S(2)}, u32[]{:S(2)}) collective-permute-start(bf16[4,48,768]{2,1,0:T(8,128)(2,1)S(1)} %stack_early.1.refs_12_.refs_1_), channel_id=1, source_target_pairs={{0,6},{1,7},{2,4},{3,5},{4,2},{5,3},{6,0},{7,1},{8,14},{9,15},{10,... | collective-permute-start | bytes 884744 | tf_op jit(solution)/shard_map/ppermute | solution.py:63
  42.6 12.9 %attention_forward.1 = (bf16[4,256,1152]{2,1,0:T(8,128)(2,1)S(1)}, bf16[4,6,256,256]{3,2,1,0:T(8,128)(2,1)S(1)}, bf16[4,256,384]{2,1,0:T(8,128)(2,1)S(1)}, f32[4...) custom-call(s32[2]{0:T(128)S(1)} %pad_add_fusion.refs_0_, ...), custom_call_target="tpu_custom_call" | custom-call | flops 4026531840 | bytes 11288064 | tf_op jit(solution)/shard_map/attention_forward/pallas_call | solution.py:158
  56.5 2.8 %collective-permute-done.16.refs_6_ = bf16[4,4,48,768]{3,2,1,0:T(8,128)(2,1)S(1)} collective-permute-done((bf16[4,4,48,768]{3,2,1,0:T(8,128)(2,1)S(1)}, bf16[4,4,48,768]{3,2,1,0:T(8,128)(2,1)S(1)}, u32[]{:S(2)}, u32[]{:S(2)}) %collective-permute-start.16) | collective-permute-done | bytes 1179680 | tf_op jit(solution)/shard_map/ppermute | solution.py:63
  59.3 14.0 %perceptron.1 = (bf16[4,256,384]{2,1,0:T(8,128)(2,1)}, f32[4,256,384]{2,1,0:T(8,128)S(1)}, f32[4,4,384]{2,1,0:T(4,128)S(1)}, f32[4,4,48,768]{3,2,1,0:T(8,128)S(1...) custom-call(s32[2]{0:T(128)S(1)} %pad_add_fusion.refs_0_, ...), custom_call_target="tpu_custom_call" | custom-call | flops 14495514624 | bytes 11480064 | tf_op jit(solution)/shard_map/perceptron/pallas_call | solution.py:158
  73.5 2.7 %collective-permute-done.17.refs_2_ = bf16[4,4,48,768]{3,2,1,0:T(8,128)(2,1)S(1)} collective-permute-done((bf16[4,4,48,768]{3,2,1,0:T(8,128)(2,1)S(1)}, bf16[4,4,48,768]{3,2,1,0:T(8,128)(2,1)S(1)}, u32[]{:S(2)}, u32[]{:S(2)}) %collective-permute-start.17) | collective-permute-done | bytes 1179680 | tf_op jit(solution)/shard_map/ppermute | solution.py:63
  80.6 10.6 %attention_backward.1 = (bf16[4,256,1152]{2,1,0:T(8,128)(2,1)S(1)}, f32[384,384]{1,0:T(8,128)S(1)}) custom-call(s32[2]{0:T(128)S(1)} %pad_add_fusion.refs_0_, f32[4,6,384]{2,1,0:T(8,128)S(1)} %get-tuple-element.91.refs_3_.refs_1_.refs_2_, bf16[4,256,384]{2,1,0:T(8,128)(2,1)S(1)} %get-tuple-element.96.refs_2_, f32[4,256,384]{2,1,0:T(8,128)S(1)} %get-tuple-element.95.refs_3_, ...), custom_call_target="tpu_custom_call" | custom-call | flops 2617245696 | bytes 11145216 | tf_op jit(solution)/shard_map/attention_backward/pallas_call | solution.py:158
  91.2 2.5 %collective-permute-done.19 = bf16[4,48,768]{2,1,0:T(8,128)(2,1)S(1)} collective-permute-done((bf16[4,48,768]{2,1,0:T(8,128)(2,1)S(1)}, bf16[4,48,768]{2,1,0:T(8,128)(2,1)S(1)}, u32[]{:S(2)}, u32[]{:S(2)}) %collective-permute-start.19) | collective-permute-done | bytes 294944 | tf_op jit(solution)/shard_map/ppermute | solution.py:63
  93.8 6.5 %attend_backward.1 = (f32[4,256,384]{2,1,0:T(8,128)}, f32[4,4,48,384]{3,2,1,0:T(8,128)S(1)}, bf16[4,4,48,384]{3,2,1,0:T(8,128)(2,1)S(1)}, bf16[4,16,384]{2,1,0:T(8,128)(2,1)S(1)}) custom-call(s32[2]{0:T(128)S(1)} %pad_add_fusion.refs_0_, bf16[4,256,384]{2,1,0:T(8,128)(2,1)S(1)} %copy-done.18, f32[4,6,384]{2,1,0:T(8,128)S(1)} %get-tuple-element.91.refs_3_.refs_1_.refs_2_, ...), custom_call_target="tpu_custom_call" | custom-call | flops 3623878656 | bytes 9653760 | tf_op jit(solution)/shard_map/attend_backward/pallas_call | solution.py:158
  106.9 3.4 %collective-permute-done.26.refs_3_ = bf16[48,768]{1,0:T(8,128)(2,1)S(1)} collective-permute-done((bf16[48,768]{1,0:T(8,128)(2,1)S(1)}, bf16[48,768]{1,0:T(8,128)(2,1)S(1)}, u32[]{:S(2)}, u32[]{:S(2)}) %collective-permute-start.26) | collective-permute-done | bytes 73760 | tf_op jit(solution)/shard_map/ppermute | solution.py:58
  115.1 2.6 %collective-permute-start.28 = (bf16[64,384]{1,0:T(8,128)(2,1)S(1)}, bf16[64,384]{1,0:T(8,128)(2,1)S(1)}, u32[]{:S(2)}, u32[]{:S(2)}) collective-permute-start(bf16[64,384]{1,0:T(8,128)(2,1)S(1)} %get-tuple-element.121), channel_id=1, source_target_pairs={{0,8},{8,16},{16,24},{24,0},{1,9},{9,17},{17,25},{25,1},{2,10},{10... | collective-permute-start | bytes 147464 | tf_op jit(solution)/shard_map/ppermute | solution.py:58
  124.2 2.6 %collective-permute-start.39 = (bf16[112,384]{1,0:T(8,128)(2,1)S(1)}, bf16[112,384]{1,0:T(8,128)(2,1)S(1)}, u32[]{:S(2)}, u32[]{:S(2)}) collective-permute-start(bf16[112,384]{1,0:T(8,128)(2,1)S(1)} %get-tuple-element.129), channel_id=1, source_target_pairs={{0,6},{1,7},{2,4},{3,5},{4,2},{5,3},{6,0},{7,1},{8,14},{9,15},{10,... | collective-permute-start | bytes 258056 | tf_op jit(solution)/shard_map/ppermute | solution.py:63
  136.1 3.3 %collective-permute-start.44 = (f32[192,128]{1,0:T(8,128)S(1)}, f32[192,128]{1,0:T(8,128)S(1)}, u32[]{:S(2)}, u32[]{:S(2)}) collective-permute-start(f32[192,128]{1,0:T(8,128)S(1)} %get-tuple-element.155), channel_id=1, source_target_pairs={{0,24},{8,0},{16,8},{24,16},{1,25},{9,1},{17,9},{25,17},{2,26},{10... | collective-permute-start | bytes 294920 | tf_op jit(solution)/shard_map/ppermute | solution.py:58
  144.4 4.0 %collective-permute-done.43 = f32[192,128]{1,0:T(8,128)S(1)} collective-permute-done((f32[192,128]{1,0:T(8,128)S(1)}, f32[192,128]{1,0:T(8,128)S(1)}, u32[]{:S(2)}, u32[]{:S(2)}) %collective-permute-start.43) | collective-permute-done | bytes 98336 | tf_op jit(solution)/shard_map/ppermute | solution.py:58
  151.0 3.4 %momenta.1 = (f32[288,384]{1,0:T(8,128)}, f32[96,384]{1,0:T(8,128)}, f32[384,384]{1,0:T(8,128)}, f32[384,384]{1,0:T(8,128)}, f32[576,384]{1,0:T(8,128)}, /*index...) custom-call(s32[2]{0:T(128)S(1)} %pad_add_fusion.refs_0_, ...), custom_call_target="tpu_custom_call" | custom-call | flops 56623104 | bytes 9252864 | tf_op jit(solution)/shard_map/momenta/pallas_call | solution.py:158
  154.3 4.9 %collective-permute-done.46.refs_3_ = f32[192,128]{1,0:T(8,128)S(1)} collective-permute-done((f32[192,128]{1,0:T(8,128)S(1)}, f32[192,128]{1,0:T(8,128)S(1)}, u32[]{:S(2)}, u32[]{:S(2)}) %collective-permute-start.46) | collective-permute-done | bytes 98336 | tf_op jit(solution)/shard_map/ppermute | solution.py:58
  159.2 11.2 %polynomial.1 = bf16[288,384]{1,0:T(8,128)(2,1)S(1)} custom-call(s32[2]{0:T(128)S(1)} %pad_add_fusion.refs_0_, f32[192,128]{1,0:T(8,128)S(1)} %fusion.1.refs_1_, f32[192,128]{1,0:T(8,128)S(1)} %collective-permute-done.45.refs_2_, f32[192,128]{1,0:T(8,128)S(1)} %collective-permute-done.46.refs_3_, f32[192,128]{1,0:T(8,128)S(1)} %collective-permute-done.47.refs_4_, ...), custom_call_target="tpu_custom_call" | custom-call | flops 6115295232 | bytes 1056768 | tf_op jit(solution)/shard_map/polynomial/pallas_call | solution.py:158
  174.0 5.7 %collective-permute-done.50 = bf16[288,384]{1,0:T(8,128)(2,1)S(1)} collective-permute-done((bf16[288,384]{1,0:T(8,128)(2,1)S(1)}, bf16[288,384]{1,0:T(8,128)(2,1)S(1)}, u32[]{:S(2)}, u32[]{:S(2)}) %collective-permute-start.50) | collective-permute-done | bytes 221216 | tf_op jit(solution)/shard_map/ppermute | solution.py:63
  179.7 3.1 %collective-permute-done.49 = bf16[288,384]{1,0:T(8,128)(2,1)S(1)} collective-permute-done((bf16[288,384]{1,0:T(8,128)(2,1)S(1)}, bf16[288,384]{1,0:T(8,128)(2,1)S(1)}, u32[]{:S(2)}, u32[]{:S(2)}) %collective-permute-start.49) | collective-permute-done | bytes 221216 | tf_op jit(solution)/shard_map/ppermute | solution.py:63
  186.3 3.6 %update.1 = (f32[288,384]{1,0:T(8,128)}, f32[96,384]{1,0:T(8,128)}, f32[384,384]{1,0:T(8,128)}, f32[384,384]{1,0:T(8,128)}, f32[576,384]{1,0:T(8,128)}) custom-call(s32[2]{0:T(128)S(1)} %pad_add_fusion.refs_0_, bf16[4,288,384]{2,1,0:T(8,128)(2,1)S(1)} %pad_maximum_fusion.refs_1_, bf16[4,288,384]{2,1,0:T(8,128)(2,1)} %collective-permute-done.51.refs_2_, ...), custom_call_target="tpu_custom_call" | custom-call | flops 1327104 | bytes 7077888 | tf_op jit(solution)/shard_map/update/pallas_call | solution.py:158
  (154 shorter events, 66.5 us)
Async XLA Ops:
  4.7 12.8 %collective-permute-start.2 = (bf16[64,384]{1,0:T(8,128)(2,1)S(1)}, bf16[64,384]{1,0:T(8,128)(2,1)S(1)}, u32[]{:S(2)}, u32[]{:S(2)}) collective-permute-start(bf16[64,384]{1,0:T(8,128)(2,1)S(1)} %prepare.1.refs_1_.refs_8_.refs_5_), channel_id=1, source_target_pairs={{0,24},{8,0},{16,8},{24,16},{1,25},{9,1},{17,9},{25,17},{2,26},{10... | collective-permute-start | bytes 147464 | tf_op jit(solution)/shard_map/ppermute | solution.py:58
  12.5 11.4 %collective-permute-start.5 = (bf16[48,768]{1,0:T(8,128)(2,1)S(1)}, bf16[48,768]{1,0:T(8,128)(2,1)S(1)}, u32[]{:S(2)}, u32[]{:S(2)}) collective-permute-start(bf16[48,768]{1,0:T(8,128)(2,1)S(1)} %pack.1.refs_1_), channel_id=1, source_target_pairs={{0,24},{8,0},{16,8},{24,16},{1,25},{9,1},{17,9},{25,17},{2,26},{10... | collective-permute-start | bytes 221192 | tf_op jit(solution)/shard_map/ppermute | solution.py:58
  13.0 10.9 %collective-permute-start.4 = (bf16[48,768]{1,0:T(8,128)(2,1)S(1)}, bf16[48,768]{1,0:T(8,128)(2,1)S(1)}, u32[]{:S(2)}, u32[]{:S(2)}) collective-permute-start(bf16[48,768]{1,0:T(8,128)(2,1)S(1)} %pack.1.refs_1_), channel_id=1, source_target_pairs={{0,16},{8,24},{16,0},{24,8},{1,17},{9,25},{17,1},{25,9},{2,18},{10... | collective-permute-start | bytes 221192 | tf_op jit(solution)/shard_map/ppermute | solution.py:58
  13.0 10.9 %collective-permute-start.3 = (bf16[48,768]{1,0:T(8,128)(2,1)S(1)}, bf16[48,768]{1,0:T(8,128)(2,1)S(1)}, u32[]{:S(2)}, u32[]{:S(2)}) collective-permute-start(bf16[48,768]{1,0:T(8,128)(2,1)S(1)} %pack.1.refs_1_), channel_id=1, source_target_pairs={{0,8},{8,16},{16,24},{24,0},{1,9},{9,17},{17,25},{25,1},{2,10},{10... | collective-permute-start | bytes 221192 | tf_op jit(solution)/shard_map/ppermute | solution.py:58
  14.6 9.3 %collective-permute-start.1 = (bf16[64,384]{1,0:T(8,128)(2,1)S(1)}, bf16[64,384]{1,0:T(8,128)(2,1)S(1)}, u32[]{:S(2)}, u32[]{:S(2)}) collective-permute-start(bf16[64,384]{1,0:T(8,128)(2,1)S(1)} %prepare.1.refs_1_.refs_8_.refs_5_), channel_id=1, source_target_pairs={{0,16},{8,24},{16,0},{24,8},{1,17},{9,25},{17,1},{25,9},{2,18},{10... | collective-permute-start | bytes 147464 | tf_op jit(solution)/shard_map/ppermute | solution.py:58
  25.1 12.7 %collective-permute-start.8 = (bf16[4,48,384]{2,1,0:T(8,128)(2,1)S(1)}, bf16[4,48,384]{2,1,0:T(8,128)(2,1)S(1)}, u32[]{:S(2)}, u32[]{:S(2)}) collective-permute-start(bf16[4,48,384]{2,1,0:T(8,128)(2,1)S(1)} %get-tuple-element.85.refs_1_), channel_id=1, source_target_pairs={{0,6},{1,7},{2,4},{3,5},{4,2},{5,3},{6,0},{7,1},{8,14},{9,15},{10,... | collective-permute-start | bytes 442376 | tf_op jit(solution)/shard_map/ppermute | solution.py:63
  27.6 10.2 %collective-permute-start.7 = (bf16[4,48,384]{2,1,0:T(8,128)(2,1)S(1)}, bf16[4,48,384]{2,1,0:T(8,128)(2,1)S(1)}, u32[]{:S(2)}, u32[]{:S(2)}) collective-permute-start(bf16[4,48,384]{2,1,0:T(8,128)(2,1)S(1)} %get-tuple-element.85.refs_1_), channel_id=1, source_target_pairs={{0,4},{1,5},{2,6},{3,7},{4,0},{5,1},{6,2},{7,3},{8,12},{9,13},{10,... | collective-permute-start | bytes 442376 | tf_op jit(solution)/shard_map/ppermute | solution.py:63
  28.1 9.7 %collective-permute-start.6 = (bf16[4,48,384]{2,1,0:T(8,128)(2,1)S(1)}, bf16[4,48,384]{2,1,0:T(8,128)(2,1)S(1)}, u32[]{:S(2)}, u32[]{:S(2)}) collective-permute-start(bf16[4,48,384]{2,1,0:T(8,128)(2,1)S(1)} %get-tuple-element.85.refs_1_), channel_id=1, source_target_pairs={{0,2},{1,3},{2,0},{3,1},{4,6},{5,7},{6,4},{7,5},{8,10},{9,11},{10,... | collective-permute-start | bytes 442376 | tf_op jit(solution)/shard_map/ppermute | solution.py:63
  39.0 16.5 %collective-permute-start.15 = (bf16[4,48,768]{2,1,0:T(8,128)(2,1)S(1)}, bf16[4,48,768]{2,1,0:T(8,128)(2,1)S(1)}, u32[]{:S(2)}, u32[]{:S(2)}) collective-permute-start(bf16[4,48,768]{2,1,0:T(8,128)(2,1)S(1)} %stack_early.1.refs_12_.refs_1_), channel_id=1, source_target_pairs={{0,6},{1,7},{2,4},{3,5},{4,2},{5,3},{6,0},{7,1},{8,14},{9,15},{10,... | collective-permute-start | bytes 884744 | tf_op jit(solution)/shard_map/ppermute | solution.py:63
  41.5 14.2 %collective-permute-start.14 = (bf16[4,48,768]{2,1,0:T(8,128)(2,1)S(1)}, bf16[4,48,768]{2,1,0:T(8,128)(2,1)S(1)}, u32[]{:S(2)}, u32[]{:S(2)}) collective-permute-start(bf16[4,48,768]{2,1,0:T(8,128)(2,1)S(1)} %stack_early.1.refs_12_.refs_1_), channel_id=1, source_target_pairs={{0,4},{1,5},{2,6},{3,7},{4,0},{5,1},{6,2},{7,3},{8,12},{9,13},{10,... | collective-permute-start | bytes 884744 | tf_op jit(solution)/shard_map/ppermute | solution.py:63
  42.0 13.8 %collective-permute-start.13 = (bf16[4,48,768]{2,1,0:T(8,128)(2,1)S(1)}, bf16[4,48,768]{2,1,0:T(8,128)(2,1)S(1)}, u32[]{:S(2)}, u32[]{:S(2)}) collective-permute-start(bf16[4,48,768]{2,1,0:T(8,128)(2,1)S(1)} %stack_early.1.refs_12_.refs_1_), channel_id=1, source_target_pairs={{0,2},{1,3},{2,0},{3,1},{4,6},{5,7},{6,4},{7,5},{8,10},{9,11},{10,... | collective-permute-start | bytes 884744 | tf_op jit(solution)/shard_map/ppermute | solution.py:63
  77.0 14.2 %collective-permute-start.18 = (bf16[4,48,768]{2,1,0:T(8,128)(2,1)S(1)}, bf16[4,48,768]{2,1,0:T(8,128)(2,1)S(1)}, u32[]{:S(2)}, u32[]{:S(2)}) collective-permute-start(bf16[4,48,768]{2,1,0:T(8,128)(2,1)S(1)} %get-tuple-element.102.refs_7_), channel_id=1, source_target_pairs={{0,2},{1,3},{2,0},{3,1},{4,6},{5,7},{6,4},{7,5},{8,10},{9,11},{10,... | collective-permute-start | bytes 884744 | tf_op jit(solution)/shard_map/ppermute | solution.py:63
  78.6 15.1 %collective-permute-start.19 = (bf16[4,48,768]{2,1,0:T(8,128)(2,1)S(1)}, bf16[4,48,768]{2,1,0:T(8,128)(2,1)S(1)}, u32[]{:S(2)}, u32[]{:S(2)}) collective-permute-start(bf16[4,48,768]{2,1,0:T(8,128)(2,1)S(1)} %get-tuple-element.103.refs_8_), channel_id=1, source_target_pairs={{0,4},{1,5},{2,6},{3,7},{4,0},{5,1},{6,2},{7,3},{8,12},{9,13},{10,... | collective-permute-start | bytes 884744 | tf_op jit(solution)/shard_map/ppermute | solution.py:63
  80.0 13.6 %collective-permute-start.20 = (bf16[4,48,768]{2,1,0:T(8,128)(2,1)S(1)}, bf16[4,48,768]{2,1,0:T(8,128)(2,1)S(1)}, u32[]{:S(2)}, u32[]{:S(2)}) collective-permute-start(bf16[4,48,768]{2,1,0:T(8,128)(2,1)S(1)} %get-tuple-element.104.refs_9_), channel_id=1, source_target_pairs={{0,6},{1,7},{2,4},{3,5},{4,2},{5,3},{6,0},{7,1},{8,14},{9,15},{10,... | collective-permute-start | bytes 884744 | tf_op jit(solution)/shard_map/ppermute | solution.py:63
  103.3 10.3 %collective-permute-start.22 = (bf16[4,48,384]{2,1,0:T(8,128)(2,1)S(1)}, bf16[4,48,384]{2,1,0:T(8,128)(2,1)S(1)}, u32[]{:S(2)}, u32[]{:S(2)}) collective-permute-start(bf16[4,48,384]{2,1,0:T(8,128)(2,1)S(1)} %get-tuple-element.116.refs_5_), channel_id=1, source_target_pairs={{0,2},{1,3},{2,0},{3,1},{4,6},{5,7},{6,4},{7,5},{8,10},{9,11},{10,... | collective-permute-start | bytes 442376 | tf_op jit(solution)/shard_map/ppermute | solution.py:63
  104.5 9.9 %collective-permute-start.23 = (bf16[4,48,384]{2,1,0:T(8,128)(2,1)S(1)}, bf16[4,48,384]{2,1,0:T(8,128)(2,1)S(1)}, u32[]{:S(2)}, u32[]{:S(2)}) collective-permute-start(bf16[4,48,384]{2,1,0:T(8,128)(2,1)S(1)} %get-tuple-element.117.refs_6_), channel_id=1, source_target_pairs={{0,4},{1,5},{2,6},{3,7},{4,0},{5,1},{6,2},{7,3},{8,12},{9,13},{10,... | collective-permute-start | bytes 442376 | tf_op jit(solution)/shard_map/ppermute | solution.py:63
  105.3 9.1 %collective-permute-start.24 = (bf16[4,48,384]{2,1,0:T(8,128)(2,1)S(1)}, bf16[4,48,384]{2,1,0:T(8,128)(2,1)S(1)}, u32[]{:S(2)}, u32[]{:S(2)}) collective-permute-start(bf16[4,48,384]{2,1,0:T(8,128)(2,1)S(1)} %get-tuple-element.118.refs_7_), channel_id=1, source_target_pairs={{0,6},{1,7},{2,4},{3,5},{4,2},{5,3},{6,0},{7,1},{8,14},{9,15},{10,... | collective-permute-start | bytes 442376 | tf_op jit(solution)/shard_map/ppermute | solution.py:63
  139.4 9.0 %collective-permute-start.43 = (f32[192,128]{1,0:T(8,128)S(1)}, f32[192,128]{1,0:T(8,128)S(1)}, u32[]{:S(2)}, u32[]{:S(2)}) collective-permute-start(f32[192,128]{1,0:T(8,128)S(1)} %get-tuple-element.156), channel_id=1, source_target_pairs={{0,16},{8,24},{16,0},{24,8},{1,17},{9,25},{17,1},{25,9},{2,18},{10... | collective-permute-start | bytes 294920 | tf_op jit(solution)/shard_map/ppermute | solution.py:58
  139.4 10.9 %collective-permute-start.34 = (f32[4,384]{1,0:T(4,128)S(1)}, f32[4,384]{1,0:T(4,128)S(1)}, u32[]{:S(2)}, u32[]{:S(2)}) collective-permute-start(f32[4,384]{1,0:T(4,128)S(1)} %get-tuple-element.126), channel_id=1, source_target_pairs={{0,24},{8,0},{16,8},{24,16},{1,25},{9,1},{17,9},{25,17},{2,26},{10... | collective-permute-start | bytes 18440 | tf_op jit(solution)/shard_map/ppermute | solution.py:58
  140.5 10.4 %collective-permute-start.35 = (f32[4,384]{1,0:T(4,128)S(1)}, f32[4,384]{1,0:T(4,128)S(1)}, u32[]{:S(2)}, u32[]{:S(2)}) collective-permute-start(f32[4,384]{1,0:T(4,128)S(1)} %get-tuple-element.127), channel_id=1, source_target_pairs={{0,16},{8,24},{16,0},{24,8},{1,17},{9,25},{17,1},{25,9},{2,18},{10... | collective-permute-start | bytes 18440 | tf_op jit(solution)/shard_map/ppermute | solution.py:58
  150.3 8.9 %collective-permute-start.46 = (f32[192,128]{1,0:T(8,128)S(1)}, f32[192,128]{1,0:T(8,128)S(1)}, u32[]{:S(2)}, u32[]{:S(2)}) collective-permute-start(f32[192,128]{1,0:T(8,128)S(1)} %fusion.1.refs_1_), channel_id=1, source_target_pairs={{0,16},{8,24},{16,0},{24,8},{1,17},{9,25},{17,1},{25,9},{2,18},{10... | collective-permute-start | bytes 294920 | tf_op jit(solution)/shard_map/ppermute | solution.py:58
  170.5 9.3 %collective-permute-start.50 = (bf16[288,384]{1,0:T(8,128)(2,1)S(1)}, bf16[288,384]{1,0:T(8,128)(2,1)S(1)}, u32[]{:S(2)}, u32[]{:S(2)}) collective-permute-start(bf16[288,384]{1,0:T(8,128)(2,1)S(1)} %polynomial.1), channel_id=1, source_target_pairs={{0,6},{1,7},{2,4},{3,5},{4,2},{5,3},{6,0},{7,1},{8,14},{9,15},{10,... | collective-permute-start | bytes 663560 | tf_op jit(solution)/shard_map/ppermute | solution.py:63
  171.1 11.7 %collective-permute-start.49 = (bf16[288,384]{1,0:T(8,128)(2,1)S(1)}, bf16[288,384]{1,0:T(8,128)(2,1)S(1)}, u32[]{:S(2)}, u32[]{:S(2)}) collective-permute-start(bf16[288,384]{1,0:T(8,128)(2,1)S(1)} %polynomial.1), channel_id=1, source_target_pairs={{0,4},{1,5},{2,6},{3,7},{4,0},{5,1},{6,2},{7,3},{8,12},{9,13},{10,... | collective-permute-start | bytes 663560 | tf_op jit(solution)/shard_map/ppermute | solution.py:63
  172.4 11.1 %collective-permute-start.48 = (bf16[288,384]{1,0:T(8,128)(2,1)S(1)}, bf16[288,384]{1,0:T(8,128)(2,1)S(1)}, u32[]{:S(2)}, u32[]{:S(2)}) collective-permute-start(bf16[288,384]{1,0:T(8,128)(2,1)S(1)} %polynomial.1), channel_id=1, source_target_pairs={{0,2},{1,3},{2,0},{3,1},{4,6},{5,7},{6,4},{7,5},{8,10},{9,11},{10,... | collective-permute-start | bytes 663560 | tf_op jit(solution)/shard_map/ppermute | solution.py:63
  (49 other events, 389.4 us)
